TPU v7x, 128 devices: a whole 4x4x4 slice. The times are simulated.
128 devices in a mesh: fsdp: 32 (over y, z, core), dp: 4 (over x).
Axes of the slice: x: 4, y: 4, z: 4, core: 2. Of those that a mesh axis runs over, the one named last changes fastest.
Arguments:
- tokens: bfloat16 [512, 202, 768], P(('fsdp', 'dp')), may hold values from -6 to 6
- lengths: int32 [512], P(('fsdp', 'dp')), may hold values from 10 to 202, as said below
- feature_proj: bfloat16 [64, 32], replicated, may hold values from -0.75 to 0.75
- ln1_gain: bfloat16 [768], P('fsdp'), may hold values from 0.5 to 1.5
- ln1_bias: bfloat16 [768], P('fsdp'), may hold values from -1 to 1
- w_query: bfloat16 [768, 768], P('fsdp'), may hold values from -0.21875 to 0.21875
- b_query: bfloat16 [768], P('fsdp'), may hold values from -1 to 1
- w_key: bfloat16 [768, 768], P('fsdp'), may hold values from -0.21875 to 0.21875
- b_key: bfloat16 [768], P('fsdp'), may hold values from -1 to 1
- w_value: bfloat16 [768, 768], P('fsdp'), may hold values from -0.21875 to 0.21875
- b_value: bfloat16 [768], P('fsdp'), may hold values from -1 to 1
- w_out: bfloat16 [768, 768], P('fsdp'), may hold values from -1.75 to 1.75
- b_out: bfloat16 [768], P('fsdp'), may hold values from -1 to 1
- ln2_gain: bfloat16 [768], P('fsdp'), may hold values from 0.5 to 1.5
- ln2_bias: bfloat16 [768], P('fsdp'), may hold values from -1 to 1
- w_up: bfloat16 [768, 3072], P('fsdp'), may hold values from -0.21875 to 0.21875
- b_up: bfloat16 [3072], P('fsdp'), may hold values from -1 to 1
- w_down: bfloat16 [3072, 768], P('fsdp'), may hold values from -0.109375 to 0.109375
- b_down: bfloat16 [768], P('fsdp'), may hold values from -1 to 1
- cotangent: bfloat16 [512, 202, 768], P(('fsdp', 'dp')), may hold values from -24 to 24
Outputs:
- layer_out: bfloat16 [512, 202, 768], P(('fsdp', 'dp'))
- grad_tokens: bfloat16 [512, 202, 768], P(('fsdp', 'dp'))
- grad_ln1_gain: float32 [768], P('fsdp')
- grad_ln1_bias: float32 [768], P('fsdp')
- grad_w_query: float32 [768, 768], P('fsdp')
- grad_b_query: float32 [768], P('fsdp')
- grad_w_key: float32 [768, 768], P('fsdp')
- grad_b_key: float32 [768], P('fsdp')
- grad_w_value: float32 [768, 768], P('fsdp')
- grad_b_value: float32 [768], P('fsdp')
- grad_w_out: float32 [768, 768], P('fsdp')
- grad_b_out: float32 [768], P('fsdp')
- grad_ln2_gain: float32 [768], P('fsdp')
- grad_ln2_bias: float32 [768], P('fsdp')
- grad_w_up: float32 [768, 3072], P('fsdp')
- grad_b_up: float32 [3072], P('fsdp')
- grad_w_down: float32 [3072, 768], P('fsdp')
- grad_b_down: float32 [768], P('fsdp')
Inputs may be any that keep to these rules, and one draw needn't show every extreme that they name: `lengths`: every molecule has 10 to 202 tokens, and at least one has exactly 202.
All inputs are finite; a program needn't handle non-finite values.
Results may differ from a plain program's by a relative error of at most 0.024.
Values may be sent and summed in bfloat16 or wider, within the bound.
A program may use at most 192 MiB of HBM per device.

v0:
```python
from functools import partial

import jax
import jax.numpy as jnp
from jax import lax
from jax.sharding import PartitionSpec as P

HEADS = 12


EPS_NORM = 1e-05
EPS_ATTN = 1e-06
HIGH = lax.Precision.HIGHEST


def normalize(inputs, gain, shift):
    centre = inputs - jnp.mean(inputs, axis=-1, keepdims=True)
    scale = lax.rsqrt(jnp.mean(centre * centre, axis=-1, keepdims=True) + EPS_NORM)
    return centre * scale * gain + shift


def attend(query, key_rows, value_rows, projection, key_mask):
    mol_count, slot_count = key_mask.shape
    model_width = query.shape[-1]
    head_size = model_width // HEADS
    half_size = head_size // 2
    positions = jnp.arange(slot_count).astype(jnp.float32)
    frequency = 10000.0 ** (jnp.arange(half_size).astype(jnp.float32) * (-2.0 / head_size))
    angles = positions[:, None] * frequency[None, :]
    cosines = jnp.cos(angles)[None, :, None, :]
    sines = jnp.sin(angles)[None, :, None, :]

    def turned(rows_in):
        heads_in = rows_in.reshape(mol_count, slot_count, HEADS, head_size)
        low_half = heads_in[..., :half_size]
        high_half = heads_in[..., half_size:]
        return jnp.concatenate(
            [low_half * cosines - high_half * sines, high_half * cosines + low_half * sines],
            axis=-1,
        )

    feat_query = jax.nn.softplus(
        jnp.einsum("gshd,df->gshf", turned(query), projection, precision=HIGH)
    )
    feat_key = jax.nn.softplus(
        jnp.einsum("gshd,df->gshf", turned(key_rows), projection, precision=HIGH)
    )
    feat_key = feat_key * key_mask[:, :, None, None]
    value_heads = value_rows.reshape(mol_count, slot_count, HEADS, head_size)
    kv_state = jnp.einsum("gshf,gshd->ghfd", feat_key, value_heads, precision=HIGH)
    feature_sum = jnp.sum(feat_key, axis=1)
    numerator = jnp.einsum("gshf,ghfd->gshd", feat_query, kv_state, precision=HIGH)
    denominator = jnp.einsum("gshf,ghf->gsh", feat_query, feature_sum, precision=HIGH) + EPS_ATTN
    return (numerator / denominator[..., None]).reshape(mol_count * slot_count, model_width)


def gelu_tanh(values):
    return jax.nn.gelu(values, approximate=True)


def matmul(left, right):
    return jnp.dot(left, right, preferred_element_type=jnp.float32)


def outer_product(left, right):
    return lax.dot_general(
        left, right, (((0,), (0,)), ((), ())), preferred_element_type=jnp.float32
    )


def times_transpose(left, right):
    return lax.dot_general(
        left, right, (((1,), (1,)), ((), ())), preferred_element_type=jnp.float32
    )


def column_sums(rows_in):
    return jnp.sum(rows_in.astype(jnp.float32), axis=0)


def body(
    tokens,
    lengths,
    feature_proj,
    ln1_gain,
    ln1_bias,
    w_query,
    b_query,
    w_key,
    b_key,
    w_value,
    b_value,
    w_out,
    b_out,
    ln2_gain,
    ln2_bias,
    w_up,
    b_up,
    w_down,
    b_down,
    cotangent,
):
    gathered = (
        lax.all_gather(ln1_gain, "fsdp", axis=0, tiled=True),
        lax.all_gather(ln1_bias, "fsdp", axis=0, tiled=True),
        lax.all_gather(w_query, "fsdp", axis=0, tiled=True),
        lax.all_gather(b_query, "fsdp", axis=0, tiled=True),
        lax.all_gather(w_key, "fsdp", axis=0, tiled=True),
        lax.all_gather(b_key, "fsdp", axis=0, tiled=True),
        lax.all_gather(w_value, "fsdp", axis=0, tiled=True),
        lax.all_gather(b_value, "fsdp", axis=0, tiled=True),
        lax.all_gather(w_out, "fsdp", axis=0, tiled=True),
        lax.all_gather(b_out, "fsdp", axis=0, tiled=True),
        lax.all_gather(ln2_gain, "fsdp", axis=0, tiled=True),
        lax.all_gather(ln2_bias, "fsdp", axis=0, tiled=True),
        lax.all_gather(w_up, "fsdp", axis=0, tiled=True),
        lax.all_gather(b_up, "fsdp", axis=0, tiled=True),
        lax.all_gather(w_down, "fsdp", axis=0, tiled=True),
        lax.all_gather(b_down, "fsdp", axis=0, tiled=True),
    )
    mol_count, slot_count, model_width = tokens.shape
    projection = feature_proj.astype(jnp.float32)
    positions = jnp.arange(slot_count, dtype=jnp.int32)
    batch_most = jnp.max(lengths)
    key_mask = (positions[None, :] < lengths[:, None]).astype(jnp.float32)
    row_flat = jnp.broadcast_to(
        (positions < batch_most).astype(jnp.float32)[None, :], (mol_count, slot_count)
    ).reshape(-1)
    gain_one = gathered[0].astype(jnp.float32)
    shift_one = gathered[1].astype(jnp.float32)
    gain_two = gathered[10].astype(jnp.float32)
    shift_two = gathered[11].astype(jnp.float32)
    flat_rows = tokens.reshape(-1, model_width).astype(jnp.float32)
    normed_one, pull_one = jax.vjp(normalize, flat_rows, gain_one, shift_one)
    lowered_one = normed_one.astype(jnp.bfloat16)
    query = matmul(lowered_one, gathered[2]) + gathered[3].astype(jnp.float32)
    key_rows = matmul(lowered_one, gathered[4]) + gathered[5].astype(jnp.float32)
    value_rows = matmul(lowered_one, gathered[6]) + gathered[7].astype(jnp.float32)
    mixed, pull_attn = jax.vjp(
        partial(attend, projection=projection, key_mask=key_mask), query, key_rows, value_rows
    )
    mixed_low = mixed.astype(jnp.bfloat16)
    middle = flat_rows + matmul(mixed_low, gathered[8]) + gathered[9].astype(jnp.float32)
    normed_two, pull_two = jax.vjp(normalize, middle, gain_two, shift_two)
    lowered_two = normed_two.astype(jnp.bfloat16)
    pre_act = matmul(lowered_two, gathered[12]) + gathered[13].astype(jnp.float32)
    activated, pull_gelu = jax.vjp(gelu_tanh, pre_act)
    hidden = activated.astype(jnp.bfloat16)
    result = (middle + matmul(hidden, gathered[14]) + gathered[15].astype(jnp.float32)) * row_flat[
        :, None
    ]
    layer_out = result.astype(jnp.bfloat16).reshape(tokens.shape)
    regathered = (
        lax.all_gather(ln1_gain, "fsdp", axis=0, tiled=True),
        lax.all_gather(ln1_bias, "fsdp", axis=0, tiled=True),
        lax.all_gather(w_query, "fsdp", axis=0, tiled=True),
        lax.all_gather(b_query, "fsdp", axis=0, tiled=True),
        lax.all_gather(w_key, "fsdp", axis=0, tiled=True),
        lax.all_gather(b_key, "fsdp", axis=0, tiled=True),
        lax.all_gather(w_value, "fsdp", axis=0, tiled=True),
        lax.all_gather(b_value, "fsdp", axis=0, tiled=True),
        lax.all_gather(w_out, "fsdp", axis=0, tiled=True),
        lax.all_gather(b_out, "fsdp", axis=0, tiled=True),
        lax.all_gather(ln2_gain, "fsdp", axis=0, tiled=True),
        lax.all_gather(ln2_bias, "fsdp", axis=0, tiled=True),
        lax.all_gather(w_up, "fsdp", axis=0, tiled=True),
        lax.all_gather(b_up, "fsdp", axis=0, tiled=True),
        lax.all_gather(w_down, "fsdp", axis=0, tiled=True),
        lax.all_gather(b_down, "fsdp", axis=0, tiled=True),
    )
    grad_out = cotangent.reshape(-1, model_width).astype(jnp.float32) * row_flat[:, None]
    grad_down = grad_out.astype(jnp.bfloat16)
    term_w_down = outer_product(hidden, grad_down)
    term_b_down = column_sums(grad_down)
    grad_hidden = times_transpose(grad_down, regathered[14])
    (grad_pre,) = pull_gelu(grad_hidden)
    grad_pre_low = grad_pre.astype(jnp.bfloat16)
    term_w_up = outer_product(lowered_two, grad_pre_low)
    term_b_up = column_sums(grad_pre_low)
    grad_two = times_transpose(grad_pre_low, regathered[12])
    grad_mid_norm, term_ln2_gain, term_ln2_bias = pull_two(grad_two)
    grad_middle = grad_out + grad_mid_norm
    grad_branch = grad_middle.astype(jnp.bfloat16)
    term_w_out = outer_product(mixed_low, grad_branch)
    term_b_out = column_sums(grad_branch)
    grad_mixed = times_transpose(grad_branch, regathered[8])
    grad_query, grad_key, grad_value = pull_attn(grad_mixed)
    query_low = grad_query.astype(jnp.bfloat16)
    key_low = grad_key.astype(jnp.bfloat16)
    value_low = grad_value.astype(jnp.bfloat16)
    term_w_query = outer_product(lowered_one, query_low)
    term_b_query = column_sums(query_low)
    term_w_key = outer_product(lowered_one, key_low)
    term_b_key = column_sums(key_low)
    term_w_value = outer_product(lowered_one, value_low)
    term_b_value = column_sums(value_low)
    grad_one = (
        times_transpose(query_low, regathered[2])
        + times_transpose(key_low, regathered[4])
        + times_transpose(value_low, regathered[6])
    )
    grad_in_norm, term_ln1_gain, term_ln1_bias = pull_one(grad_one)
    grad_tokens = (grad_middle + grad_in_norm).astype(jnp.bfloat16).reshape(tokens.shape)
    (
        part_a,
        part_b,
        part_c,
        part_d,
        part_e,
        part_f,
        part_g,
        part_h,
        part_i,
        part_j,
        part_k,
        part_l,
        part_m,
        part_n,
        part_o,
        part_p,
    ) = (
        lax.psum_scatter(
            term_ln1_gain.astype(jnp.bfloat16), "fsdp", scatter_dimension=0, tiled=True
        ).astype(jnp.float32),
        lax.psum_scatter(
            term_ln1_bias.astype(jnp.bfloat16), "fsdp", scatter_dimension=0, tiled=True
        ).astype(jnp.float32),
        lax.psum_scatter(
            term_w_query.astype(jnp.bfloat16), "fsdp", scatter_dimension=0, tiled=True
        ).astype(jnp.float32),
        lax.psum_scatter(
            term_b_query.astype(jnp.bfloat16), "fsdp", scatter_dimension=0, tiled=True
        ).astype(jnp.float32),
        lax.psum_scatter(
            term_w_key.astype(jnp.bfloat16), "fsdp", scatter_dimension=0, tiled=True
        ).astype(jnp.float32),
        lax.psum_scatter(
            term_b_key.astype(jnp.bfloat16), "fsdp", scatter_dimension=0, tiled=True
        ).astype(jnp.float32),
        lax.psum_scatter(
            term_w_value.astype(jnp.bfloat16), "fsdp", scatter_dimension=0, tiled=True
        ).astype(jnp.float32),
        lax.psum_scatter(
            term_b_value.astype(jnp.bfloat16), "fsdp", scatter_dimension=0, tiled=True
        ).astype(jnp.float32),
        lax.psum_scatter(
            term_w_out.astype(jnp.bfloat16), "fsdp", scatter_dimension=0, tiled=True
        ).astype(jnp.float32),
        lax.psum_scatter(
            term_b_out.astype(jnp.bfloat16), "fsdp", scatter_dimension=0, tiled=True
        ).astype(jnp.float32),
        lax.psum_scatter(
            term_ln2_gain.astype(jnp.bfloat16), "fsdp", scatter_dimension=0, tiled=True
        ).astype(jnp.float32),
        lax.psum_scatter(
            term_ln2_bias.astype(jnp.bfloat16), "fsdp", scatter_dimension=0, tiled=True
        ).astype(jnp.float32),
        lax.psum_scatter(
            term_w_up.astype(jnp.bfloat16), "fsdp", scatter_dimension=0, tiled=True
        ).astype(jnp.float32),
        lax.psum_scatter(
            term_b_up.astype(jnp.bfloat16), "fsdp", scatter_dimension=0, tiled=True
        ).astype(jnp.float32),
        lax.psum_scatter(
            term_w_down.astype(jnp.bfloat16), "fsdp", scatter_dimension=0, tiled=True
        ).astype(jnp.float32),
        lax.psum_scatter(
            term_b_down.astype(jnp.bfloat16), "fsdp", scatter_dimension=0, tiled=True
        ).astype(jnp.float32),
    )
    summed = (
        lax.psum(part_a.astype(jnp.bfloat16), "dp").astype(jnp.float32),
        lax.psum(part_b.astype(jnp.bfloat16), "dp").astype(jnp.float32),
        lax.psum(part_c.astype(jnp.bfloat16), "dp").astype(jnp.float32),
        lax.psum(part_d.astype(jnp.bfloat16), "dp").astype(jnp.float32),
        lax.psum(part_e.astype(jnp.bfloat16), "dp").astype(jnp.float32),
        lax.psum(part_f.astype(jnp.bfloat16), "dp").astype(jnp.float32),
        lax.psum(part_g.astype(jnp.bfloat16), "dp").astype(jnp.float32),
        lax.psum(part_h.astype(jnp.bfloat16), "dp").astype(jnp.float32),
        lax.psum(part_i.astype(jnp.bfloat16), "dp").astype(jnp.float32),
        lax.psum(part_j.astype(jnp.bfloat16), "dp").astype(jnp.float32),
        lax.psum(part_k.astype(jnp.bfloat16), "dp").astype(jnp.float32),
        lax.psum(part_l.astype(jnp.bfloat16), "dp").astype(jnp.float32),
        lax.psum(part_m.astype(jnp.bfloat16), "dp").astype(jnp.float32),
        lax.psum(part_n.astype(jnp.bfloat16), "dp").astype(jnp.float32),
        lax.psum(part_o.astype(jnp.bfloat16), "dp").astype(jnp.float32),
        lax.psum(part_p.astype(jnp.bfloat16), "dp").astype(jnp.float32),
    )
    return (
        layer_out,
        grad_tokens,
        summed[0],
        summed[1],
        summed[2],
        summed[3],
        summed[4],
        summed[5],
        summed[6],
        summed[7],
        summed[8],
        summed[9],
        summed[10],
        summed[11],
        summed[12],
        summed[13],
        summed[14],
        summed[15],
    )


def solution(mesh):
    placed = (
        P(("fsdp", "dp"), None, None),
        P(("fsdp", "dp")),
        P(),
        P("fsdp"),
        P("fsdp"),
        P("fsdp", None),
        P("fsdp"),
        P("fsdp", None),
        P("fsdp"),
        P("fsdp", None),
        P("fsdp"),
        P("fsdp", None),
        P("fsdp"),
        P("fsdp"),
        P("fsdp"),
        P("fsdp", None),
        P("fsdp"),
        P("fsdp", None),
        P("fsdp"),
        P(("fsdp", "dp"), None, None),
    )
    return jax.shard_map(
        body,
        mesh=mesh,
        in_specs=placed,
        out_specs=(
            P(("fsdp", "dp"), None, None),
            P(("fsdp", "dp"), None, None),
            P("fsdp"),
            P("fsdp"),
            P("fsdp", None),
            P("fsdp"),
            P("fsdp", None),
            P("fsdp"),
            P("fsdp", None),
            P("fsdp"),
            P("fsdp", None),
            P("fsdp"),
            P("fsdp"),
            P("fsdp"),
            P("fsdp", None),
            P("fsdp"),
            P("fsdp", None),
            P("fsdp"),
        ),
        check_vma=False,
    )
```

profile of v0, /device:TPU:1, one launch (start us, length us, event | category | flops | bytes accessed | tf_op | source)
XLA Modules:
  0.0 952.1 jit_solution(3698323063060429159)
XLA Ops:
  20.4 125.9 %all-reduce.25 = (bf16[768]{0:T(1024)(128)(2,1)S(1)}, bf16[768]{0:T(1024)(128)(2,1)S(1)}, bf16[768]{0:T(1024)(128)(2,1)S(1)}, bf16[768]{0:T(1024)(128)(2,1)S(1)}...) all-reduce(bf16[768]{0:T(1024)(128)(2,1)S(1)} %dynamic-update-slice, ...), channel_id=1, replica_groups=mesh['fsdp'=32,'dp'=4] {'fsdp'}, use_global_device_ids=true, to_apply=%add.5 | all-reduce | flops 9216 | bytes 36864
  178.7 11.5 %fusion.89 = (f32[4,202,12,32]{3,2,1,0:T(8,128)}, f32[4,202,12,32]{3,2,1,0:T(8,128)}) fusion(f32[4,202,12,64]{3,2,1,0:T(8,128)} %reshape.399), kind=kLoop, calls=%fused_computation.163 | loop fusion | bytes 4964352 | tf_op jit(solution)/shard_map/jvp()/slice | solution.py:36
  190.2 5.7 copy.130
  195.9 5.7 copy.129
  205.8 5.5 reshape.397
  211.4 11.5 %fusion.90 = (f32[4,202,12,32]{3,2,1,0:T(8,128)}, f32[4,202,12,32]{3,2,1,0:T(8,128)}) fusion(f32[4,202,12,64]{3,2,1,0:T(8,128)} %reshape.397), kind=kLoop, calls=%fused_computation.164 | loop fusion | bytes 4964352 | tf_op jit(solution)/shard_map/jvp()/slice | solution.py:36
  222.8 5.7 copy.127
  228.5 5.8 copy.128
  244.1 6.5 copy.98
  265.4 5.6 fusion.19
  286.0 11.1 %fusion.84 = f32[808,3072]{1,0:T(8,128)} fusion(bf16[768,3072]{1,0:T(8,128)(2,1)} %all-gather.15.cloned.1.call-done, f32[808,768]{1,0:T(8,128)} %copy-done.9, f32[768]{0:T(1024)} %convert_element_type.347, f32[768]{0:T(1024)} %convert_element_type.346, f32[808]{0:T(1024)} %fusion.66, f32[808]{0:T(1024)S(1)} %broadcast_multiply_fusion.1), kind=kOutput, calls=%fused_computation.158 | convolution fusion | flops 3815725056 | bytes 17142080 | tf_op jit(solution)/shard_map/dot_general | solution.py:62
  297.2 14.9 %fusion.94 = (bf16[3072]{0:T(1024)(128)(2,1)}, bf16[808,3072]{1,0:T(8,128)(2,1)S(1)}) fusion(f32[808,3072]{1,0:T(8,128)} %fusion.84, f32[3072]{0:T(1024)S(1)} %copy-done.43, bf16[3072,768]{1,0:T(8,128)(2,1)} %all-gather.17.cloned.1.call-done, f32[808,768]{1,0:T(8,128)} %reshape.331, f32[808]{0:T(1024)S(1)} %mul.536), kind=kOutput, calls=%fused_computation.168 | convolution fusion | flops 3868468224 | bytes 22115488 | tf_op jit(solution)/shard_map/dot_general | solution.py:72
  324.2 5.9 reshape.328
  330.2 6.6 fusion.15
  398.2 9.9 %convolution_convert_fusion.1 = bf16[768,3072]{1,0:T(8,128)(2,1)} fusion(bf16[808,3072]{1,0:T(8,128)(2,1)} %copy-done.67, f32[808,768]{1,0:T(8,128)} %copy-done.9, f32[768]{0:T(1024)S(1)} %copy-done.47, f32[768]{0:T(1024)S(1)} %copy-done.40, f32[808]{0:T(1024)S(1)} %copy-done.42, f32[808]{0:T(1024)S(1)} %broadcast_multiply_fusion.1), kind=kOutput, calls=%fused_computation.11 | convolution fusion | flops 3818084352 | bytes 12177728 | tf_op jit(solution)/shard_map/dot_general | solution.py:66
  408.8 12.4 %convolution_convert_fusion = bf16[3072,768]{1,0:T(8,128)(2,1)} fusion(f32[808,768]{1,0:T(8,128)} %reshape.331, f32[808]{0:T(1024)S(1)} %mul.536, f32[808,3072]{1,0:T(8,128)} %fusion.84, f32[3072]{0:T(1024)S(1)} %copy-done.44), kind=kOutput, calls=%fused_computation.10 | convolution fusion | flops 3841044480 | bytes 17144992 | tf_op jit(solution)/shard_map/dot_general | solution.py:66
  433.8 124.1 %all-reduce.24 = (bf16[768]{0:T(1024)(128)(2,1)S(1)}, bf16[768]{0:T(1024)(128)(2,1)S(1)}, bf16[768]{0:T(1024)(128)(2,1)S(1)}, bf16[768]{0:T(1024)(128)(2,1)S(1)}...) all-reduce(bf16[768]{0:T(1024)(128)(2,1)S(1)} %dynamic-update-slice, ...), channel_id=1, replica_groups=mesh['fsdp'=32,'dp'=4] {'fsdp'}, use_global_device_ids=true, to_apply=%add.13 | all-reduce | flops 10752 | bytes 43008
  557.9 11.5 %multiply_convert_fusion.2 = bf16[808,768]{1,0:T(8,128)(2,1)} fusion(f32[808,768]{1,0:T(8,128)} %copy-done.9, bf16[3072,768]{1,0:T(8,128)(2,1)} %all-gather.17.cloned.1.call-done, f32[808]{0:T(1024)S(1)} %mul.536, f32[768]{0:T(1024)S(1)} %convert_element_type.351, f32[808,3072]{1,0:T(8,128)} %fusion.84, f32[3072]{0:T(1024)S(1)} %copy-done.44), kind=kOutput, calls=%fused_computation.44 | convolution fusion | flops 3839926272 | bytes 18389152 | tf_op jit(solution)/shard_map/dot_general | solution.py:62
  583.4 15.1 %reduce-scatter.11.cloned.1.call-done = bf16[24,768]{1,0:T(8,128)(2,1)} async-done(((bf16[768,768]{1,0:T(8,128)(2,1)}), bf16[24,768]{1,0:T(8,128)(2,1)}) %reduce-scatter.11.cloned.1.call-update) | async-done | bytes 36880 | tf_op jit(solution)/shard_map/reduce_scatter | solution.py:240
  598.5 78.7 %reduce-scatter.13.cloned.1.call-done = bf16[24,768]{1,0:T(8,128)(2,1)} async-done(((bf16[768,768]{1,0:T(8,128)(2,1)}), bf16[24,768]{1,0:T(8,128)(2,1)}) %reduce-scatter.13.cloned.1.call-update) | async-done | bytes 36880 | tf_op jit(solution)/shard_map/reduce_scatter | solution.py:246
  677.3 86.6 %reduce-scatter.15.cloned.1.call-done = bf16[24,3072]{1,0:T(8,128)(2,1)} async-done(((bf16[768,3072]{1,0:T(8,128)(2,1)}), bf16[24,3072]{1,0:T(8,128)(2,1)}) %reduce-scatter.15.cloned.1.call-update) | async-done | bytes 147472 | tf_op jit(solution)/shard_map/reduce_scatter | solution.py:258
  763.9 87.0 %reduce-scatter.17.cloned.1.call-done = bf16[96,768]{1,0:T(8,128)(2,1)} async-done(((bf16[3072,768]{1,0:T(8,128)(2,1)}), bf16[96,768]{1,0:T(8,128)(2,1)}) %reduce-scatter.17.cloned.1.call-update) | async-done | bytes 147472 | tf_op jit(solution)/shard_map/reduce_scatter | solution.py:264
  855.7 42.2 %all-reduce.31.cloned.1.call-done = (bf16[24]{0:T(256)(128)(2,1)}, bf16[24]{0:T(256)(128)(2,1)}, bf16[24,768]{1,0:T(8,128)(2,1)}, bf16[24]{0:T(256)(128)(2,1)}, ...) async-done(((bf16[24]{0:T(256)(128)(2,1)}, ...) | async-done | bytes 148096 | tf_op jit(solution)/shard_map/psum | solution.py:272
  915.1 27.0 %all-reduce.33.cloned.1.call-done = (bf16[24,3072]{1,0:T(8,128)(2,1)}, bf16[96,768]{1,0:T(8,128)(2,1)}) async-done(((bf16[24,3072]{1,0:T(8,128)(2,1)}, bf16[96,768]{1,0:T(8,128)(2,1)}), (bf16[24,3072]{1,0:T(8,128)(2,1)}, bf16[96,768]{1,0:T(8,128)(2,1)})) %all-reduce.33.cloned.1.call-update) | async-done | bytes 294928 | tf_op jit(solution)/shard_map/psum | solution.py:284
  (318 shorter events, 212.2 us)
Async XLA Ops:
  7.2 247.2 %copy-start = (bf16[64,32]{0,1:T(8,128)(2,1)S(1)}, bf16[64,32]{0,1:T(8,128)(2,1)}, u32[]{:S(2)}) copy-start(bf16[64,32]{0,1:T(8,128)(2,1)} %param.23) | copy-start | bytes 12292
  7.2 161.7 %all-gather.11.cloned.1.call-start = ((), (), s32[]{:S(2)}) async-start(), calls=%async_computation.8 | async-start | bytes 1216512 | tf_op jit(solution)/shard_map/all_gather | solution.py:106
  7.9 193.6 %all-gather.7.cloned.1.call-start = ((), (), s32[]{:S(2)}) async-start(), calls=%async_computation.6 | async-start | bytes 1216512 | tf_op jit(solution)/shard_map/all_gather | solution.py:108
  8.7 225.6 %all-gather.9.cloned.1.call-start = ((), (), s32[]{:S(2)}) async-start(), calls=%async_computation.7 | async-start | bytes 1216512 | tf_op jit(solution)/shard_map/all_gather | solution.py:110
  9.4 268.1 %all-gather.13.cloned.1.call-start = ((), (), s32[]{:S(2)}) async-start(), calls=%async_computation.9 | async-start | bytes 1216512 | tf_op jit(solution)/shard_map/all_gather | solution.py:112
  10.0 276.0 %all-gather.15.cloned.1.call-start = ((), (), s32[]{:S(2)}) async-start(), calls=%async_computation.10 | async-start | bytes 4866048 | tf_op jit(solution)/shard_map/all_gather | solution.py:116
  10.6 286.6 %all-gather.17.cloned.1.call-start = ((), (), s32[]{:S(2)}) async-start(), calls=%async_computation.11 | async-start | bytes 4866048 | tf_op jit(solution)/shard_map/all_gather | solution.py:118
  11.2 572.2 %reduce-scatter.7.cloned.1.call-start = ((), (), s32[]{:S(2)}) async-start(), calls=%async_computation.12 | async-start | bytes 1216512 | tf_op jit(solution)/shard_map/reduce_scatter | solution.py:228
  148.3 19.1 %copy-start.25 = (f32[768]{0:T(1024)}, f32[768]{0:T(1024)S(1)}, u32[]{:S(2)}) copy-start(f32[768]{0:T(1024)S(1)} %convert_element_type.334) | copy-start | bytes 9220
  148.5 18.9 %copy-start.31 = (f32[808]{0:T(1024)}, f32[808]{0:T(1024)S(1)}, u32[]{:S(2)}) copy-start(f32[808]{0:T(1024)S(1)} %rsqrt.23) | copy-start | bytes 9700
  148.6 18.8 %copy-start.33 = (f32[808]{0:T(1024)}, f32[808]{0:T(1024)S(1)}, u32[]{:S(2)}) copy-start(f32[808]{0:T(1024)S(1)} %div.57) | copy-start | bytes 9700
  286.0 11.2 %copy-start.43 = (f32[3072]{0:T(1024)S(1)}, f32[3072]{0:T(1024)}, u32[]{:S(2)}) copy-start(f32[3072]{0:T(1024)} %convert_element_type.349) | copy-start | bytes 36868
  297.1 14.9 %copy-start.39 = (f32[768]{0:T(1024)S(1)}, f32[768]{0:T(1024)}, u32[]{:S(2)}) copy-start(f32[768]{0:T(1024)} %convert_element_type.346) | copy-start | bytes 9220
  297.1 14.9 %copy-start.41 = (f32[808]{0:T(1024)S(1)}, f32[808]{0:T(1024)}, u32[]{:S(2)}) copy-start(f32[808]{0:T(1024)} %fusion.66) | copy-start | bytes 9700
  297.1 14.9 %copy-start.10 = (f32[808,768]{1,0:T(8,128)S(1)}, f32[808,768]{1,0:T(8,128)}, u32[]{:S(2)}) copy-start(f32[808,768]{1,0:T(8,128)} %copy-done.9) | copy-start | bytes 7446532
  297.2 14.9 %copy-start.54 = (bf16[768,3072]{1,0:T(8,128)(2,1)S(1)}, bf16[768,3072]{1,0:T(8,128)(2,1)}, u32[]{:S(2)}) copy-start(bf16[768,3072]{1,0:T(8,128)(2,1)} %all-gather.15.cloned.1.call-done) | copy-start | bytes 14155780
  364.7 218.7 %reduce-scatter.9.cloned.1.call-start = ((), (), s32[]{:S(2)}) async-start(), calls=%async_computation.13 | async-start | bytes 1216512 | tf_op jit(solution)/shard_map/reduce_scatter | solution.py:234
  377.1 221.4 %reduce-scatter.11.cloned.1.call-start = ((), (), s32[]{:S(2)}) async-start(), calls=%async_computation.14 | async-start | bytes 1216512 | tf_op jit(solution)/shard_map/reduce_scatter | solution.py:240
  393.5 283.7 %reduce-scatter.13.cloned.1.call-start = ((), (), s32[]{:S(2)}) async-start(), calls=%async_computation.15 | async-start | bytes 1216512 | tf_op jit(solution)/shard_map/reduce_scatter | solution.py:246
  398.2 365.7 %reduce-scatter.15.cloned.1.call-start = ((), (), s32[]{:S(2)}) async-start(), calls=%async_computation.16 | async-start | bytes 4866048 | tf_op jit(solution)/shard_map/reduce_scatter | solution.py:258
  408.1 442.8 %reduce-scatter.17.cloned.1.call-start = ((), (), s32[]{:S(2)}) async-start(), calls=%async_computation.17 | async-start | bytes 4866048 | tf_op jit(solution)/shard_map/reduce_scatter | solution.py:264
  421.2 476.6 %all-reduce.31.cloned.1.call-start = ((), (), s32[]{:S(2)}) async-start(), calls=%async_computation.18 | async-start | bytes 305152 | tf_op jit(solution)/shard_map/psum | solution.py:272
  572.0 9.0 copy-start.11
  677.3 264.8 %all-reduce.33.cloned.1.call-start = ((), (), s32[]{:S(2)}) async-start(), calls=%async_computation.19 | async-start | bytes 589824 | tf_op jit(solution)/shard_map/psum | solution.py:284
  (58 other events, 200.3 us)
Sparse Core Ops, SparseCore 0:
  10.4 46.7 all-gather.10
  59.5 42.2 all-gather.6
  104.1 42.2 all-gather.8
  148.7 42.3 all-gather.12
  193.1 46.1 all-gather.14
  241.5 46.2 all-gather.16
  364.8 75.7 reduce-scatter.6
  444.1 75.4 reduce-scatter.8
  523.1 75.3 reduce-scatter.10
  601.9 75.2 reduce-scatter.12
  681.0 82.8 reduce-scatter.14
  767.9 82.9 reduce-scatter.16
  856.0 41.8 all-reduce.30
  900.2 41.8 all-reduce.32
where the time goes:
time: 959 us; the launch traced here: 952 us
  waiting for transfers between devices  340 us (35%)
  blocking collectives  250 us (26%)
  matrix products  148 us (15%)
  local copies, waits for them, and re-layouts  142 us (15%)
  other arithmetic  52 us (5%)
  between operations  17.7 us (2%)
    unnamed x2, blocking collectives  250 us
    reduce_scatter x1, waiting for transfers between devices, body(): lax.psum_scatter(term_w_down.astype(jnp.bfloat16), 'fsdp', scatter_dimens...  87 us
    reduce_scatter x1, waiting for transfers between devices, body(): lax.psum_scatter(term_w_up.astype(jnp.bfloat16), 'fsdp', scatter_dimensio...  86.6 us
    reduce_scatter x1, waiting for transfers between devices, body(): lax.psum_scatter(term_w_out.astype(jnp.bfloat16), 'fsdp', scatter_dimensi...  78.7 us
    unnamed x174, local copies, waits for them, and re-layouts  42.3 us
    psum x1, waiting for transfers between devices, body(): lax.psum(part_a.astype(jnp.bfloat16), 'dp').astype(jnp.float32)  42.2 us
    dot_general x6, matrix products, outer_product(): lax.dot_general(left, right, (((0,), (0,)), ((), ())), preferred_element_...  39.6 us
    dot_general x6, matrix products, matmul(): return jnp.dot(left, right, preferred_element_type=jnp.float32)  38.6 us
  transfers between devices with their start and end apart: 14, of which 6 were waited for; matrix products, arithmetic and copies ran while one was open for 28% of the time, Pallas kernels for 0%

commit v1 on v0

v1 whole, which is shorter than its diff:
```python
from functools import partial

import jax
import jax.numpy as jnp
from jax import lax
from jax.experimental import pallas as pl
from jax.experimental.pallas import tpu as pltpu
from jax.sharding import PartitionSpec as P

HEADS = 12


MESH = pl.DeviceIdType.MESH
RING = 4
BLK = 48
WID = 768
HALF = 384
ALL = pl.ds(0, RING)


def rounded(value):
    return value.astype(jnp.bfloat16)


def wide(value):
    return value.astype(jnp.float32)


class Net:
    def __init__(self, send_sems, recv_sems):
        self.send_sems, self.recv_sems, self.count, self.open = send_sems, recv_sems, 0, []
        index = lax.axis_index("fsdp")
        self.x = lax.axis_index("dp")
        self.y = index // (2 * RING)
        self.z = (index // 2) % RING
        self.c = index % 2

    def at(self, y, z, c):
        return {"fsdp": ((y + RING) % RING) * (2 * RING) + ((z + RING) % RING) * 2 + c}

    def sibling(self):
        return self.at(self.y, self.z, 1 - self.c)

    def along(self, axis, step):
        if axis == "y":
            return self.at(self.y + step, self.z, self.c)
        if axis == "z":
            return self.at(self.y, self.z + step, self.c)
        return {"dp": (self.x + step) % RING}

    def greet(self):
        barrier = pltpu.get_barrier_semaphore()
        peers = [self.sibling()] + [
            self.along(axis, step) for axis in ("x", "y", "z") for step in (1, 2, 3)
        ]
        for peer in peers:
            pl.semaphore_signal(barrier, inc=1, device_id=peer, device_id_type=MESH)
        pl.semaphore_wait(barrier, len(peers))

    def send(self, src, dst, device):
        slot = self.count
        self.count += 1
        copy = pltpu.make_async_remote_copy(
            src_ref=src,
            dst_ref=dst,
            send_sem=self.send_sems.at[slot],
            recv_sem=self.recv_sems.at[slot],
            device_id=device,
            device_id_type=MESH,
        )
        copy.start()
        self.open.append(copy)
        return slot

    def arrived(self, slot, land):
        pltpu.make_async_remote_copy(
            src_ref=land,
            dst_ref=land,
            send_sem=self.send_sems.at[slot],
            recv_sem=self.recv_sems.at[slot],
            device_id=self.sibling(),
            device_id_type=MESH,
        ).wait_recv()

    def settle(self):
        for copy in self.open:
            copy.wait_send()
        self.open = []

    def axes(self, way):
        return ("y", "z") if way == 0 else ("z", "y")

    def place(self, way):
        return (self.y, self.z) if way == 0 else (self.z, self.y)


def wrap(index):
    return (index + RING) % RING


def slot_of(ref, part, way, core, first, second):
    y, z = (first, second) if way == 0 else (second, first)
    piece = 2 * core + way
    if part < 2:
        return ref.at[4 * part + piece, y, z]
    if not isinstance(y, pl.Slice):
        return ref.at[8 + y, z, piece]
    return ref.at[pl.ds(8, RING), z, piece]


def half(ref, side):
    lead = (slice(None),) * (len(ref.shape) - 1)
    return ref.at[lead + (pl.ds(side * HALF, HALF),)]


def gather_steps(net, weights, part):
    ways = (0, 1)
    sent = {}

    def slot(way, first, second, core=None):
        return slot_of(weights, part, way, net.c if core is None else core, first, second)

    for way in ways:
        p, q = net.place(way)
        axis = net.axes(way)[0]
        own = slot(way, p, q)
        sent[way, "r"] = net.send(own, own, net.along(axis, 1))
        sent[way, "l"] = net.send(own, own, net.along(axis, -1))
    yield
    for way in ways:
        p, q = net.place(way)
        axis = net.axes(way)[0]
        left = slot(way, wrap(p - 1), q)
        net.arrived(sent[way, "r"], left)
        sent[way, "fr"] = net.send(half(left, 0), half(left, 0), net.along(axis, 1))
        right = slot(way, wrap(p + 1), q)
        net.arrived(sent[way, "l"], right)
        sent[way, "fl"] = net.send(half(right, 1), half(right, 1), net.along(axis, -1))
    yield
    for way in ways:
        p, q = net.place(way)
        axis = net.axes(way)[1]
        far = slot(way, wrap(p + 2), q)
        net.arrived(sent[way, "fr"], half(far, 0))
        net.arrived(sent[way, "fl"], half(far, 1))
        row = slot(way, ALL, q)
        sent[way, "r2"] = net.send(row, row, net.along(axis, 1))
        sent[way, "l2"] = net.send(row, row, net.along(axis, -1))
        sent[way, "s0"] = net.send(row, row, net.sibling())
    yield
    for way in ways:
        p, q = net.place(way)
        axis = net.axes(way)[1]
        left = slot(way, ALL, wrap(q - 1))
        net.arrived(sent[way, "r2"], left)
        sent[way, "fr2"] = net.send(half(left, 0), half(left, 0), net.along(axis, 1))
        sent[way, "s1"] = net.send(left, left, net.sibling())
        right = slot(way, ALL, wrap(q + 1))
        net.arrived(sent[way, "l2"], right)
        sent[way, "fl2"] = net.send(half(right, 1), half(right, 1), net.along(axis, -1))
        sent[way, "s2"] = net.send(right, right, net.sibling())
    yield
    for way in ways:
        p, q = net.place(way)
        far = slot(way, ALL, wrap(q + 2))
        net.arrived(sent[way, "fr2"], half(far, 0))
        net.arrived(sent[way, "fl2"], half(far, 1))
        sent[way, "s3"] = net.send(far, far, net.sibling())
    yield
    for way in ways:
        p, q = net.place(way)
        other = 1 - net.c
        for name, step in (("s0", 0), ("s1", -1), ("s2", 1), ("s3", 2)):
            net.arrived(sent[way, name], slot(way, ALL, wrap(q + step), other))


def gather_small(net, small):
    own = small.at[net.y, net.z]
    sent = [net.send(own, own, net.along("y", step)) for step in (1, 2, 3)]
    yield
    for slot, step in zip(sent, (1, 2, 3)):
        net.arrived(slot, small.at[wrap(net.y - step), net.z])
    row = small.at[ALL, net.z]
    sent = [net.send(row, row, net.along("z", step)) for step in (1, 2, 3)]
    yield
    for slot, step in zip(sent, (1, 2, 3)):
        net.arrived(slot, small.at[ALL, wrap(net.z - step)])


def load_shards(net, weights, small, mine, theirs, small_mine, shards):
    queries, keys, values, outs, ups, downs, packed = shards
    first = net.c == 0
    rows = pl.ds(pl.multiple_of(24 * net.c, 8), 24)

    def lane(piece):
        return pl.ds(pl.multiple_of(WID * piece, WID), WID)

    for way in (0, 1):
        early, late = ((queries, values), (keys, outs))[way]
        early, late = wide(early[...]), wide(late[...])
        mine[way, rows] = jnp.where(first, early, late)
        theirs[way] = jnp.where(first, late, early)
        mine[2 + way, rows] = wide(ups[:, lane(2 * net.c + way)])
        theirs[2 + way] = wide(ups[:, lane(2 - 2 * net.c + way)])
    small_mine[rows] = wide(packed[...])
    sent = net.send(theirs, mine.at[ALL, rows], net.sibling())
    sent_small = net.send(small_mine.at[rows], small_mine.at[rows], net.sibling())
    for way in (0, 1):
        weights[8 + net.y, net.z, 2 * net.c + way] = downs[pl.ds(BLK * way, BLK)]
    others = pl.ds(pl.multiple_of(24 - 24 * net.c, 8), 24)
    net.arrived(sent_small, small_mine.at[others])
    small[net.y, net.z] = rounded(small_mine[...])
    net.arrived(sent, mine.at[ALL, others])
    for part in (0, 1):
        for way in (0, 1):
            weights[4 * part + 2 * net.c + way, net.y, net.z] = rounded(mine[2 * part + way])


def add_blocks(target, source):
    if len(target.shape) == 2:
        target[...] = rounded(wide(target[...]) + wide(source[...]))
        return
    for index in range(target.shape[0]):
        add_blocks(target.at[index], source.at[index])


def add_two(target, one, two):
    if len(target.shape) == 2:
        target[...] = rounded(wide(target[...]) + wide(one[...]) + wide(two[...]))
        return
    for index in range(target.shape[0]):
        add_two(target.at[index], one.at[index], two.at[index])


def ring_reduce(net, group, land, axis, me):
    ahead, behind, far = wrap(me + 1), wrap(me - 1), wrap(me + 2)
    right, left = net.along(axis, 1), net.along(axis, -1)
    one_r = net.send(half(group(far), 0), land.at[0], right)
    one_l = net.send(half(group(far), 1), land.at[1], left)
    two_r = net.send(half(group(ahead), 1), land.at[2], right)
    two_l = net.send(half(group(behind), 0), land.at[3], left)
    yield
    net.arrived(one_r, land.at[0])
    add_blocks(half(group(ahead), 0), land.at[0])
    three_r = net.send(half(group(ahead), 0), land.at[4], right)
    net.arrived(one_l, land.at[1])
    add_blocks(half(group(behind), 1), land.at[1])
    three_l = net.send(half(group(behind), 1), land.at[5], left)
    yield
    net.arrived(two_r, land.at[2])
    net.arrived(three_l, land.at[5])
    add_two(half(group(me), 1), land.at[2], land.at[5])
    net.arrived(two_l, land.at[3])
    net.arrived(three_r, land.at[4])
    add_two(half(group(me), 0), land.at[3], land.at[4])


def together(*steps):
    steps = list(steps)
    while steps:
        steps = [step for step in steps if next(step, steps) is not steps]
        if steps:
            yield


def reduce_steps(net, grads, part, pair, big, little, cross, total, result):
    ways = (0, 1)

    def slot(way, first, second):
        return slot_of(grads, part, way, net.c, first, second)

    def whole(way, core):
        if part < 2:
            return grads.at[4 * part + 2 * core + way]
        return grads.at[pl.ds(8, RING), ALL, 2 * core + way]

    sent = [net.send(whole(way, 1 - net.c), pair.at[way], net.sibling()) for way in ways]
    yield
    for way in ways:
        net.arrived(sent[way], pair.at[way])
        for index in range(RING):
            add_blocks(whole(way, net.c).at[index], pair.at[way, index])
    yield from together(
        *[
            ring_reduce(
                net,
                lambda at, way=way: slot(way, ALL, at),
                big.at[way],
                net.axes(way)[1],
                net.place(way)[1],
            )
            for way in ways
        ]
    )
    yield
    yield from together(
        *[
            ring_reduce(
                net,
                lambda at, way=way: slot(way, at, net.place(way)[1]),
                little.at[way],
                net.axes(way)[0],
                net.place(way)[0],
            )
            for way in ways
        ]
    )
    sent = {}
    for way in ways:
        cross[way, net.x] = slot(way, *net.place(way))[...]
        for step in (1, 2, 3):
            mine = cross.at[way, net.x]
            sent[way, step] = net.send(mine, mine, net.along("x", step))
    yield
    for way in ways:
        for step in (1, 2, 3):
            net.arrived(sent[way, step], cross.at[way, wrap(net.x - step)])
        total[way] = (
            (wide(cross[way, 0]) + wide(cross[way, 1])) + wide(cross[way, 2])
        ) + wide(cross[way, 3])
    if part == 2:
        for way in ways:
            result[pl.ds(BLK * way, BLK)] = total[way]
        return
    sent = []
    for way in ways:
        mine = result.at[2 * net.c + way]
        result[2 * net.c + way] = total[way, pl.ds(pl.multiple_of(24 * net.c, 8), 24)]
        sent.append(
            net.send(
                total.at[way, pl.ds(pl.multiple_of(24 - 24 * net.c, 8), 24)], mine, net.sibling()
            )
        )
    yield
    for way in ways:
        net.arrived(sent[way], result.at[2 - 2 * net.c + way])


def vector_steps(net, vectors, land):
    sent = net.send(vectors, land.at[0, 0], net.sibling())
    yield
    net.arrived(sent, land.at[0, 0])
    value = vectors[...] + land[0, 0]
    for stage, axis, me in ((1, "z", net.z), (2, "y", net.y), (3, "x", net.x)):
        land[stage, me] = value
        mine = land.at[stage, me]
        sent = [net.send(mine, mine, net.along(axis, step)) for step in (1, 2, 3)]
        yield
        for step in (1, 2, 3):
            net.arrived(sent[step - 1], land.at[stage, wrap(me - step)])
        value = ((land[stage, 0] + land[stage, 1]) + land[stage, 2]) + land[stage, 3]
    land[0, 1] = value

VMEM = pl.BlockSpec(memory_space=pltpu.VMEM)
ANY = pl.BlockSpec(memory_space=pl.ANY)


def gather_kernel(
    queries, keys, values, outs, ups, downs, packed, weights_out, small_out,
    weights, small, mine, theirs, small_mine, send_sems, recv_sems, local_sem,
):
    net = Net(send_sems, recv_sems)
    net.greet()
    load_shards(net, weights, small, mine, theirs, small_mine, (queries, keys, values, outs, ups, downs, packed))
    steps = together(gather_small(net, small), *[gather_steps(net, weights, part) for part in (0, 1, 2)])
    for _ in steps:
        pass
    net.settle()
    copy = pltpu.make_async_copy(weights, weights_out, local_sem.at[0])
    copy.start()
    copy_small = pltpu.make_async_copy(small, small_out, local_sem.at[1])
    copy_small.start()
    copy.wait()
    copy_small.wait()


def gather_call(*shards):
    bf = jnp.bfloat16
    return pl.pallas_call(
        gather_kernel,
        out_shape=(
            jax.ShapeDtypeStruct((12, 4, 4, 48, 768), bf),
            jax.ShapeDtypeStruct((4, 4, 48, 128), bf),
        ),
        in_specs=[VMEM] * 7,
        out_specs=(ANY, ANY),
        scratch_shapes=[
            pltpu.VMEM((12, 4, 4, 48, 768), bf),
            pltpu.VMEM((4, 4, 48, 128), bf),
            pltpu.VMEM((4, 48, 768), jnp.float32),
            pltpu.VMEM((4, 24, 768), jnp.float32),
            pltpu.VMEM((48, 128), jnp.float32),
            pltpu.SemaphoreType.DMA((128,)),
            pltpu.SemaphoreType.DMA((128,)),
            pltpu.SemaphoreType.DMA((2,)),
        ],
        compiler_params=pltpu.CompilerParams(
            collective_id=0, has_side_effects=True, vmem_limit_bytes=60 * 2**20
        ),
    )(*shards)


def reduce_kernel(
    terms, vectors_in, out_square, out_up, out_down, out_vectors,
    grads, vectors, pair, big, little, cross, total, land, square, up, down,
    send_sems, recv_sems, local_sem,
):
    net = Net(send_sems, recv_sems)
    copy = pltpu.make_async_copy(terms, grads, local_sem.at[0])
    copy.start()
    vectors[...] = vectors_in[...]
    net.greet()
    copy.wait()
    steps = [
        reduce_steps(net, grads, part, pair.at[part], big.at[part], little.at[part], cross.at[part], total.at[part], result)
        for part, result in ((2, down), (1, up), (0, square))
    ]
    for _ in together(vector_steps(net, vectors, land), *steps):
        pass
    net.settle()
    out_square[...] = square[...]
    out_up[...] = up[...]
    out_down[...] = down[...]
    out_vectors[...] = land[0, 1]


def reduce_call(terms, vectors):
    bf, ff = jnp.bfloat16, jnp.float32
    return pl.pallas_call(
        reduce_kernel,
        out_shape=(
            jax.ShapeDtypeStruct((4, 24, 768), ff),
            jax.ShapeDtypeStruct((4, 24, 768), ff),
            jax.ShapeDtypeStruct((96, 768), ff),
            jax.ShapeDtypeStruct((16, 768), ff),
        ),
        in_specs=[ANY, VMEM],
        out_specs=(VMEM, VMEM, VMEM, VMEM),
        scratch_shapes=[
            pltpu.VMEM((12, 4, 4, 48, 768), bf),
            pltpu.VMEM((16, 768), ff),
            pltpu.VMEM((3, 2, 4, 4, 48, 768), bf),
            pltpu.VMEM((3, 2, 6, 4, 48, 384), bf),
            pltpu.VMEM((3, 2, 6, 48, 384), bf),
            pltpu.VMEM((3, 2, 4, 48, 768), bf),
            pltpu.VMEM((3, 2, 48, 768), ff),
            pltpu.VMEM((4, 4, 16, 768), ff),
            pltpu.VMEM((4, 24, 768), ff),
            pltpu.VMEM((4, 24, 768), ff),
            pltpu.VMEM((96, 768), ff),
            pltpu.SemaphoreType.DMA((128,)),
            pltpu.SemaphoreType.DMA((128,)),
            pltpu.SemaphoreType.DMA((2,)),
        ],
        compiler_params=pltpu.CompilerParams(
            collective_id=1, has_side_effects=True, vmem_limit_bytes=60 * 2**20
        ),
    )(terms, vectors)


EPS_NORM = 1e-05
EPS_ATTN = 1e-06
HIGH = lax.Precision.HIGHEST


def normalize(inputs, gain, shift):
    centre = inputs - jnp.mean(inputs, axis=-1, keepdims=True)
    scale = lax.rsqrt(jnp.mean(centre * centre, axis=-1, keepdims=True) + EPS_NORM)
    return centre * scale * gain + shift


def attend(query, key_rows, value_rows, projection, key_mask):
    mol_count, slot_count = key_mask.shape
    model_width = query.shape[-1]
    head_size = model_width // HEADS
    half_size = head_size // 2
    positions = jnp.arange(slot_count).astype(jnp.float32)
    frequency = 10000.0 ** (jnp.arange(half_size).astype(jnp.float32) * (-2.0 / head_size))
    angles = positions[:, None] * frequency[None, :]
    cosines = jnp.cos(angles)[None, :, None, :]
    sines = jnp.sin(angles)[None, :, None, :]

    def turned(rows_in):
        heads_in = rows_in.reshape(mol_count, slot_count, HEADS, head_size)
        low_half = heads_in[..., :half_size]
        high_half = heads_in[..., half_size:]
        return jnp.concatenate(
            [low_half * cosines - high_half * sines, high_half * cosines + low_half * sines],
            axis=-1,
        )

    feat_query = jax.nn.softplus(
        jnp.einsum("gshd,df->gshf", turned(query), projection, precision=HIGH)
    )
    feat_key = jax.nn.softplus(
        jnp.einsum("gshd,df->gshf", turned(key_rows), projection, precision=HIGH)
    )
    feat_key = feat_key * key_mask[:, :, None, None]
    value_heads = value_rows.reshape(mol_count, slot_count, HEADS, head_size)
    kv_state = jnp.einsum("gshf,gshd->ghfd", feat_key, value_heads, precision=HIGH)
    feature_sum = jnp.sum(feat_key, axis=1)
    numerator = jnp.einsum("gshf,ghfd->gshd", feat_query, kv_state, precision=HIGH)
    denominator = jnp.einsum("gshf,ghf->gsh", feat_query, feature_sum, precision=HIGH) + EPS_ATTN
    return (numerator / denominator[..., None]).reshape(mol_count * slot_count, model_width)


def gelu_tanh(values):
    return jax.nn.gelu(values, approximate=True)


def matmul(left, right):
    return jnp.dot(left, right, preferred_element_type=jnp.float32)


def outer_product(left, right):
    return lax.dot_general(
        left, right, (((0,), (0,)), ((), ())), preferred_element_type=jnp.float32
    )


def times_transpose(left, right):
    return lax.dot_general(
        left, right, (((1,), (1,)), ((), ())), preferred_element_type=jnp.float32
    )


def column_sums(rows_in):
    return jnp.sum(rows_in.astype(jnp.float32), axis=0)


def body(
    tokens,
    lengths,
    feature_proj,
    ln1_gain,
    ln1_bias,
    w_query,
    b_query,
    w_key,
    b_key,
    w_value,
    b_value,
    w_out,
    b_out,
    ln2_gain,
    ln2_bias,
    w_up,
    b_up,
    w_down,
    b_down,
    cotangent,
):
    packed = jnp.stack(
        [ln1_gain, ln1_bias, b_query, b_key, b_value, b_out, ln2_gain, ln2_bias, b_down]
        + [b_up[24 * k : 24 * k + 24] for k in range(4)],
        axis=1,
    )
    packed = jnp.pad(packed, ((0, 0), (0, 128 - 13)))
    weights, small = gather_call(w_query, w_key, w_value, w_out, w_up, w_down, packed)
    small = small.reshape(768, 128)
    squares = weights.reshape(12, 768, 768)
    full_up = jnp.concatenate([squares[4], squares[5], squares[6], squares[7]], axis=1)
    full_down = squares[8:].reshape(3072, 768)
    full_b_up = small[:, 9:13].reshape(32, 24, 4).transpose(0, 2, 1).reshape(3072)
    gathered = regathered = (
        small[:, 0], small[:, 1], squares[0], small[:, 2], squares[1], small[:, 3], squares[2], small[:, 4],
        squares[3], small[:, 5], small[:, 6], small[:, 7], full_up, full_b_up, full_down, small[:, 8],
    )
    mol_count, slot_count, model_width = tokens.shape
    projection = feature_proj.astype(jnp.float32)
    positions = jnp.arange(slot_count, dtype=jnp.int32)
    batch_most = jnp.max(lengths)
    key_mask = (positions[None, :] < lengths[:, None]).astype(jnp.float32)
    row_flat = jnp.broadcast_to(
        (positions < batch_most).astype(jnp.float32)[None, :], (mol_count, slot_count)
    ).reshape(-1)
    gain_one = gathered[0].astype(jnp.float32)
    shift_one = gathered[1].astype(jnp.float32)
    gain_two = gathered[10].astype(jnp.float32)
    shift_two = gathered[11].astype(jnp.float32)
    flat_rows = tokens.reshape(-1, model_width).astype(jnp.float32)
    normed_one, pull_one = jax.vjp(normalize, flat_rows, gain_one, shift_one)
    lowered_one = normed_one.astype(jnp.bfloat16)
    query = matmul(lowered_one, gathered[2]) + gathered[3].astype(jnp.float32)
    key_rows = matmul(lowered_one, gathered[4]) + gathered[5].astype(jnp.float32)
    value_rows = matmul(lowered_one, gathered[6]) + gathered[7].astype(jnp.float32)
    mixed, pull_attn = jax.vjp(
        partial(attend, projection=projection, key_mask=key_mask), query, key_rows, value_rows
    )
    mixed_low = mixed.astype(jnp.bfloat16)
    middle = flat_rows + matmul(mixed_low, gathered[8]) + gathered[9].astype(jnp.float32)
    normed_two, pull_two = jax.vjp(normalize, middle, gain_two, shift_two)
    lowered_two = normed_two.astype(jnp.bfloat16)
    pre_act = matmul(lowered_two, gathered[12]) + gathered[13].astype(jnp.float32)
    activated, pull_gelu = jax.vjp(gelu_tanh, pre_act)
    hidden = activated.astype(jnp.bfloat16)
    result = (middle + matmul(hidden, gathered[14]) + gathered[15].astype(jnp.float32)) * row_flat[
        :, None
    ]
    layer_out = result.astype(jnp.bfloat16).reshape(tokens.shape)
    grad_out = cotangent.reshape(-1, model_width).astype(jnp.float32) * row_flat[:, None]
    grad_down = grad_out.astype(jnp.bfloat16)
    term_w_down = outer_product(hidden, grad_down)
    term_b_down = column_sums(grad_down)
    grad_hidden = times_transpose(grad_down, regathered[14])
    (grad_pre,) = pull_gelu(grad_hidden)
    grad_pre_low = grad_pre.astype(jnp.bfloat16)
    term_w_up = outer_product(lowered_two, grad_pre_low)
    term_b_up = column_sums(grad_pre_low)
    grad_two = times_transpose(grad_pre_low, regathered[12])
    grad_mid_norm, term_ln2_gain, term_ln2_bias = pull_two(grad_two)
    grad_middle = grad_out + grad_mid_norm
    grad_branch = grad_middle.astype(jnp.bfloat16)
    term_w_out = outer_product(mixed_low, grad_branch)
    term_b_out = column_sums(grad_branch)
    grad_mixed = times_transpose(grad_branch, regathered[8])
    grad_query, grad_key, grad_value = pull_attn(grad_mixed)
    query_low = grad_query.astype(jnp.bfloat16)
    key_low = grad_key.astype(jnp.bfloat16)
    value_low = grad_value.astype(jnp.bfloat16)
    term_w_query = outer_product(lowered_one, query_low)
    term_b_query = column_sums(query_low)
    term_w_key = outer_product(lowered_one, key_low)
    term_b_key = column_sums(key_low)
    term_w_value = outer_product(lowered_one, value_low)
    term_b_value = column_sums(value_low)
    grad_one = (
        times_transpose(query_low, regathered[2])
        + times_transpose(key_low, regathered[4])
        + times_transpose(value_low, regathered[6])
    )
    grad_in_norm, term_ln1_gain, term_ln1_bias = pull_one(grad_one)
    grad_tokens = (grad_middle + grad_in_norm).astype(jnp.bfloat16).reshape(tokens.shape)
    low = lambda v: v.astype(jnp.bfloat16)
    terms = jnp.concatenate(
        [low(term_w_query)[None], low(term_w_key)[None], low(term_w_value)[None], low(term_w_out)[None]]
        + [low(term_w_up[:, 768 * j : 768 * j + 768])[None] for j in range(4)]
        + [low(term_w_down).reshape(4, 768, 768)],
        axis=0,
    ).reshape(12, 4, 4, 48, 768)
    vectors = jnp.stack(
        [term_ln1_gain, term_ln1_bias, term_b_query, term_b_key, term_b_value, term_b_out,
         term_ln2_gain, term_ln2_bias, term_b_down]
        + [term_b_up[768 * j : 768 * j + 768] for j in range(4)]
        + [jnp.zeros_like(term_b_out)] * 3
    )
    square, up, down, vectors = reduce_call(terms, vectors)
    index = lax.axis_index("fsdp")
    narrow = lax.dynamic_slice(vectors, (0, 24 * index), (9, 24))
    grad_b_up = lax.dynamic_slice(vectors[9:13].reshape(3072), (96 * index,), (96,))
    return (
        layer_out, grad_tokens, narrow[0], narrow[1], square[0], narrow[2], square[1], narrow[3], square[2], narrow[4],
        square[3], narrow[5], narrow[6], narrow[7], up.transpose(1, 0, 2).reshape(24, 3072), grad_b_up, down, narrow[8],
    )


def solution(mesh):
    placed = (
        P(("fsdp", "dp"), None, None),
        P(("fsdp", "dp")),
        P(),
        P("fsdp"),
        P("fsdp"),
        P("fsdp", None),
        P("fsdp"),
        P("fsdp", None),
        P("fsdp"),
        P("fsdp", None),
        P("fsdp"),
        P("fsdp", None),
        P("fsdp"),
        P("fsdp"),
        P("fsdp"),
        P("fsdp", None),
        P("fsdp"),
        P("fsdp", None),
        P("fsdp"),
        P(("fsdp", "dp"), None, None),
    )
    return jax.shard_map(
        body,
        mesh=mesh,
        in_specs=placed,
        out_specs=(
            P(("fsdp", "dp"), None, None),
            P(("fsdp", "dp"), None, None),
            P("fsdp"),
            P("fsdp"),
            P("fsdp", None),
            P("fsdp"),
            P("fsdp", None),
            P("fsdp"),
            P("fsdp", None),
            P("fsdp"),
            P("fsdp", None),
            P("fsdp"),
            P("fsdp"),
            P("fsdp"),
            P("fsdp", None),
            P("fsdp"),
            P("fsdp", None),
            P("fsdp"),
        ),
        check_vma=False,
    )
```

time: 959 us -> 478 us (0.50)
  waiting for transfers between devices: 340 us -> 0 us
  blocking collectives: 250 us -> 0 us
  Pallas kernels: 0 us -> 137 us
  local copies, waits for them, and re-layouts: 142 us -> 175 us
  other arithmetic: 52 us -> 29.4 us
  matrix products: 148 us -> 127 us
  between operations: 17.7 us -> 1.76 us
    reduce_scatter x6 -> x0, waiting for transfers between devices: 267 us -> none  [the longest x1 87 us: body(): lax.psum_scatter(term_w_down.astype(jnp.bfloat16), 'fsdp', scatter_dimens...]
    unnamed x2 -> x0, blocking collectives: 250 us -> none
    pallas_call x0 -> x2, Pallas kernels: none -> 137 us  [the longest x1 75.9 us: reduce_call(): pl.pallas_call(reduce_kernel, out_shape=(jax.ShapeDtypeStruct((4, 24, 768...]
    psum x2 -> x0, waiting for transfers between devices: 69.1 us -> none  [the longest x1 42.2 us: body(): lax.psum(part_a.astype(jnp.bfloat16), 'dp').astype(jnp.float32)]
    convert_element_type x18 -> x0, other arithmetic: 21.1 us -> none  [the longest x1 1.64 us: body(): lax.psum(part_m.astype(jnp.bfloat16), 'dp').astype(jnp.float32)]
    slice x0 -> x6, local copies, waits for them, and re-layouts: none -> 15.4 us  [the longest x1 6.37 us: body(): squares[4]]
    another operation x0 -> x27, local copies, waits for them, and re-layouts: none -> 10.8 us  [the longest x15 8.11 us: body(): jnp.stack([ln1_gain, ln1_bias, b_query, b_key, b_value, b_out, ln2_gain,...]
    unnamed x174 -> x141, local copies, waits for them, and re-layouts: 42.3 us -> 48.4 us
  transfers between devices with their start and end apart: 14 -> 0, of which waited for: 6 -> 0; matrix products, arithmetic and copies ran while one was open for 28% -> 0% of each run, Pallas kernels for 0% -> 0%
where the time goes in v1:
time: 478 us; the launch traced here: 470 us
  local copies, waits for them, and re-layouts  175 us (37%)
  Pallas kernels  137 us (29%)
  matrix products  127 us (27%)
  other arithmetic  29.4 us (6%)
    pallas_call x1, Pallas kernels, reduce_call(): pl.pallas_call(reduce_kernel, out_shape=(jax.ShapeDtypeStruct((4, 24, 768...  75.9 us
    pallas_call x1, Pallas kernels, gather_call(): pl.pallas_call(gather_kernel, out_shape=(jax.ShapeDtypeStruct((12, 4, 4,...  60.8 us
    unnamed x141, local copies, waits for them, and re-layouts  48.4 us
    dot_general x6, matrix products, outer_product(): lax.dot_general(left, right, (((0,), (0,)), ((), ())), preferred_element_...  33.2 us
    dot_general x6, matrix products, matmul(): return jnp.dot(left, right, preferred_element_type=jnp.float32)  29.9 us
    dot_general x6, matrix products, times_transpose(): lax.dot_general(left, right, (((1,), (1,)), ((), ())), preferred_element_...  27.5 us
    slice x2, local copies, waits for them, and re-layouts, turned(): high_half = heads_in[..., half_size:]  22.8 us
    dot_general x3, matrix products, attend(): jnp.einsum('gshf,ghfd->gshd', feat_query, kv_state, precision=HIGH)  11.8 us

profile of v1, /device:TPU:1, one launch (start us, length us, event | category | flops | bytes accessed | tf_op | source)
XLA Modules:
  0.0 469.9 jit_solution(2468197902971007163)
XLA Ops:
  32.5 60.8 %shard_map.331 = (bf16[12,4,4,48,768]{4,3,2,1,0:T(8,128)(2,1)}, bf16[4,4,48,128]{3,2,1,0:T(8,128)(2,1)}) custom-call(bf16[24,768]{1,0:T(8,128)(2,1)} %queries.1, bf16[24,768]{1,0:T(8,128)(2,1)} %keys.1, bf16[24,768]{1,0:T(8,128)(2,1)} %values.1, bf16[24,768]{1,0:T(8,128)(2,1)} %outs.1, bf16[24,3072]{1,0:T(8,128)(2,1)} %ups.1, bf16[96,768]{1,0:T(8,128)(2,1)} %downs.1, ...), custom_call_target="tpu_custom_call" | custom-call | tf_op jit(solution)/shard_map/pallas_call | solution.py:379
  99.8 5.4 %slice.185 = bf16[4,4,4,48,768]{4,3,2,1,0:T(8,128)(2,1)} slice(bf16[12,4,4,48,768]{4,3,2,1,0:T(8,128)(2,1)} %get-tuple-element.29), slice={[8:12], [0:4], [0:4], [0:48], [0:768]} | slice | bytes 9437184 | tf_op jit(solution)/shard_map/slice | solution.py:563
  105.2 6.4 %fusion.89 = (bf16[1,4,4,48,768]{4,3,2,1,0:T(8,128)(2,1)}, bf16[1,4,4,48,768]{4,3,2,1,0:T(8,128)(2,1)}, bf16[1,4,4,48,768]{4,3,2,1,0:T(8,128)(2,1)}, bf16[1,4,4,...) fusion(bf16[12,4,4,48,768]{4,3,2,1,0:T(8,128)(2,1)} %get-tuple-, ...), kind=kLoop, calls=%fused_computation.202 | loop fusion | bytes 18874368 | tf_op jit(solution)/shard_map/slice | solution.py:562
  119.5 5.5 %reshape.561 = f32[4,202,12,64]{3,2,1,0:T(8,128)} reshape(f32[808,768]{1,0:T(8,128)} %convolution_add_fusion.2) | data formatting | bytes 4964352 | tf_op jit(solution)/shard_map/jvp()/reshape | solution.py:484
  129.2 4.8 %copy.220 = f32[4,202,12,64]{1,3,2,0:T(8,128)S(1)} copy(f32[4,202,12,64]{3,2,1,0:T(8,128)} %reshape.562) | data formatting | bytes 4964352 | tf_op jit(solution)/shard_map/jvp()/reshape | solution.py:499
  133.9 5.5 %reshape.563 = f32[4,202,12,64]{3,2,1,0:T(8,128)} reshape(f32[808,768]{1,0:T(8,128)} %convolution_add_fusion) | data formatting | bytes 4964352 | tf_op jit(solution)/shard_map/jvp()/reshape | solution.py:484
  139.4 11.5 %fusion.90 = (f32[4,202,12,32]{3,2,1,0:T(8,128)}, f32[4,202,12,32]{3,2,1,0:T(8,128)}) fusion(f32[4,202,12,64]{3,2,1,0:T(8,128)} %reshape.563), kind=kLoop, calls=%fused_computation.203 | loop fusion | bytes 4964352 | tf_op jit(solution)/shard_map/jvp()/slice | solution.py:486
  150.9 5.7 %copy.261 = f32[4,202,12,32]{1,3,2,0:T(8,128)} copy(f32[4,202,12,32]{3,2,1,0:T(8,128)} %get-tuple-element.160) | data formatting | bytes 2482176
  156.6 5.7 %copy.260 = f32[4,202,12,32]{1,3,2,0:T(8,128)} copy(f32[4,202,12,32]{3,2,1,0:T(8,128)} %get-tuple-element.161) | data formatting | bytes 2482176
  162.3 11.3 %fusion.91 = (f32[4,202,12,32]{3,2,1,0:T(8,128)}, f32[4,202,12,32]{3,2,1,0:T(8,128)}) fusion(f32[4,202,12,64]{3,2,1,0:T(8,128)} %reshape.561), kind=kLoop, calls=%fused_computation.204 | loop fusion | bytes 4964352 | tf_op jit(solution)/shard_map/jvp()/slice | solution.py:486
  173.6 5.7 %copy.257 = f32[4,202,12,32]{1,3,2,0:T(8,128)} copy(f32[4,202,12,32]{3,2,1,0:T(8,128)} %get-tuple-element.162) | data formatting | bytes 2482176
  179.3 6.1 %copy.256 = f32[4,202,12,32]{1,3,2,0:T(8,128)} copy(f32[4,202,12,32]{3,2,1,0:T(8,128)} %get-tuple-element.163) | data formatting | bytes 2482176
  201.8 5.6 %fusion.15 = (bf16[4,202,12,64]{1,3,2,0:T(8,128)(2,1)S(1)}, f32[4,12,64,202]{3,2,1,0:T(8,128)}) fusion(f32[4,202,12]{1,2,0:T(8,128)S(1)} %get-tuple-element.205, f32[4,12,32,64]{3,2,1,0:T(8,128)S(1)} %fusion.81, f32[4,202,12,32]{1,3,2,0:T(8,128)S(1)} %get-tuple-element.219, u16[4,202,32]{1,2,0:T(8,128)(2,1)S(1)} %get-tuple-element.137), kind=kOutput, calls=%fused_computation.29 | convolution fusion | flops 242322432 | bytes 5448064 | tf_op jit(solution)/shard_map/jvp(gshf,ghfd->gshd)/dot_general | solution.py:502
  219.6 8.1 %fusion.43 = f32[808,3072]{1,0:T(8,128)} fusion(bf16[768,768]{1,0:T(8,128)(2,1)S(1)} %bitcast.199, bf16[768,768]{1,0:T(8,128)(2,1)S(1)} %bitcast.201, bf16[768,768]{1,0:T(8,128)(2,1)S(1)} %bitcast.203, bf16[768,768]{1,0:T(8,128)(2,1)S(1)} %bitcast.197, f32[808,768]{1,0:T(8,128)S(1)} %get-tuple-element.223, f32[768]{0:T(1024)S(1)} %get-tuple-element.232, ...), kind=kOutput, calls=%fused_computation.105 | convolution fusion | flops 3834599424 | bytes 17142080 | tf_op jit(solution)/shard_map/dot_general | solution.py:512
  227.6 10.2 %multiply_convert_fusion.2 = bf16[808,768]{1,0:T(8,128)(2,1)} fusion(f32[808,768]{1,0:T(8,128)S(1)} %get-tuple-element.223, bf16[3072,768]{1,0:T(8,128)(2,1)S(1)} %bitcast.190, f32[808]{0:T(1024)S(1)} %mul.541, f32[768]{0:T(1024)S(1)} %copy-done.55, f32[808,3072]{1,0:T(8,128)} %fusion.43, f32[3072]{0:T(1024)S(1)} %reshape.549), kind=kOutput, calls=%fused_computation.46 | convolution fusion | flops 3839926272 | bytes 18389152 | tf_op jit(solution)/shard_map/dot_general | solution.py:512
  237.8 12.3 %convert_reduce_fusion = (f32[3072]{0:T(1024)S(1)}, bf16[808,3072]{1,0:T(8,128)(2,1)S(1)}) fusion(f32[808,3072]{1,0:T(8,128)} %fusion.43, f32[3072]{0:T(1024)S(1)} %reshape.549, bf16[808,768]{1,0:T(8,128)(2,1)S(1)} %copy-done.27, bf16[3072,768]{1,0:T(8,128)(2,1)S(1)} %bitcast.191), kind=kOutput, calls=%fused_computation.9 | convolution fusion | flops 3869709312 | bytes 20877312 | tf_op jit(solution)/shard_map/dot_general | solution.py:522
  250.1 11.9 %convolution_convert_fusion = bf16[3072,768]{1,0:T(8,128)(2,1)} fusion(f32[808,768]{1,0:T(8,128)S(1)} %copy-done.1, f32[808]{0:T(1024)S(1)} %mul.541, f32[808,3072]{1,0:T(8,128)} %fusion.43, f32[3072]{0:T(1024)S(1)} %reshape.549), kind=kOutput, calls=%fused_computation.11 | convolution fusion | flops 3841044480 | bytes 17144992 | tf_op jit(solution)/shard_map/dot_general | solution.py:516
  262.0 4.5 multiply_reduce_fusion
  268.9 6.2 %convolution_convert_fusion.1 = bf16[768,3072]{1,0:T(8,128)(2,1)S(1)} fusion(bf16[808,3072]{1,0:T(8,128)(2,1)S(1)} %get-tuple-element.139, f32[808,768]{1,0:T(8,128)S(1)} %get-tuple-element.223, f32[768]{0:T(1024)S(1)} %get-tuple-element.232, f32[768]{0:T(1024)S(1)} %get-tuple-element.233, f32[808]{0:T(1024)S(1)} %fusion.67, ...), kind=kOutput, calls=%fused_computation.12 | convolution fusion | flops 3818084352 | bytes 12177728 | tf_op jit(solution)/shard_map/dot_general | solution.py:516
  309.0 5.0 %convert_reduce_fusion.1 = (f32[12,64]{1,0:T(8,128)S(1)}, bf16[4,202,12,64]{1,3,2,0:T(8,128)(2,1)}) fusion(f32[4,12,64,32]{2,3,1,0:T(8,128)S(1)} %fusion.39, f32[4,202,12,32]{1,3,2,0:T(8,128)S(1)} %copy-done.9, f32[4,202]{1,0:T(4,128)S(1)} %fusion.66, u16[4,202,32]{1,2,0:T(8,128)(2,1)S(1)} %get-tuple-element.135), kind=kOutput, calls=%fused_computation.31 | convolution fusion | flops 243252480 | bytes 2933408 | tf_op jit(solution)/shard_map/transpose(jvp(gshf,gshd->ghfd))/dot_general | solution.py:500
  323.5 4.6 convert_element_type.385
  339.0 4.4 convolution_convert_fusion.5
  380.8 5.0 %constant_dynamic-update-slice_fusion.terms = bf16[12,4,4,48,768]{4,3,2,1,0:T(8,128)(2,1)} fusion(bf16[12,4,4,48,768]{4,3,2,1,0:T(8,128)(2,1)} %constant_dynamic-update-slice_fusion.1, bf16[4,4,4,48,768]{4,3,2,1,0:T(8,128)(2,1)} %bitcast.187), kind=kLoop, calls=%fused_computation.137 | loop fusion | bytes 9437184 | tf_op jit(solution)/shard_map/concatenate | solution.py:635
  385.8 75.9 %shard_map.332 = (f32[4,24,768]{2,1,0:T(8,128)}, f32[4,24,768]{2,1,0:T(8,128)}, f32[96,768]{1,0:T(8,128)}, f32[16,768]{1,0:T(8,128)}) custom-call(bf16[12,4,4,48,768]{4,3,2,1,0:T(8,128)(2,1)} %constant_dynamic-update-slice_fusion.terms, f32[16,768]{1,0:T(8,128)} %stack.103.vectors_in), custom_call_target="tpu_custom_call" | custom-call | tf_op jit(solution)/shard_map/pallas_call | solution.py:429
  (270 shorter events, 180.3 us)
Async XLA Ops:
  0.7 188.4 %copy-start = (bf16[64,32]{0,1:T(8,128)(2,1)S(1)}, bf16[64,32]{0,1:T(8,128)(2,1)}, u32[]{:S(2)}) copy-start(bf16[64,32]{0,1:T(8,128)(2,1)} %param.23) | copy-start | bytes 12292
  0.7 15.2 %copy-start.6 = (bf16[4,202,768]{2,0,1:T(4,128)(2,1)S(1)}, bf16[4,202,768]{2,0,1:T(4,128)(2,1)}, u32[]{:S(2)}) copy-start(bf16[4,202,768]{2,0,1:T(4,128)(2,1)} %param.21) | copy-start | bytes 3723268
  13.1 4.9 %copy-start.12 = (bf16[4,202,768]{2,0,1:T(4,128)(2,1)S(1)}, bf16[4,202,768]{2,0,1:T(4,128)(2,1)}, u32[]{:S(2)}) copy-start(bf16[4,202,768]{2,0,1:T(4,128)(2,1)} %param.40) | copy-start | bytes 3723268
  99.8 11.9 %copy-start.25 = (bf16[808,768]{1,0:T(8,128)(2,1)}, bf16[808,768]{1,0:T(8,128)(2,1)S(1)}, u32[]{:S(2)}) copy-start(bf16[808,768]{1,0:T(8,128)(2,1)S(1)} %convert_element_type.344) | copy-start | bytes 3723268
  111.6 5.2 %copy-start.30 = (bf16[1,4,4,48,768]{4,3,2,1,0:T(8,128)(2,1)}, bf16[1,4,4,48,768]{4,3,2,1,0:T(8,128)(2,1)S(1)}, u32[]{:S(2)}) copy-start(bf16[1,4,4,48,768]{4,3,2,1,0:T(8,128)(2,1)S(1)} %get-tuple-element.159) | copy-start | bytes 3538948
  179.3 6.1 %copy-start.44 = (f32[202,32]{0,1:T(8,128)S(1)}, f32[202,32]{0,1:T(8,128)}, u32[]{:S(2)}) copy-start(f32[202,32]{0,1:T(8,128)} %get-tuple-element.212) | copy-start | bytes 77572
  179.3 6.1 %copy-start.45 = (f32[202,32]{0,1:T(8,128)S(1)}, f32[202,32]{0,1:T(8,128)}, u32[]{:S(2)}) copy-start(f32[202,32]{0,1:T(8,128)} %get-tuple-element.213) | copy-start | bytes 77572
  190.9 10.8 %copy-start.21 = (f32[4,202,12,32]{1,3,2,0:T(8,128)}, f32[4,202,12,32]{1,3,2,0:T(8,128)S(1)}, u32[]{:S(2)}) copy-start(f32[4,202,12,32]{1,3,2,0:T(8,128)S(1)} %get-tuple-element.219) | copy-start | bytes 3723268
  201.8 5.6 %copy-start.40 = (f32[4,12,32,64]{3,2,1,0:T(8,128)}, f32[4,12,32,64]{3,2,1,0:T(8,128)S(1)}, u32[]{:S(2)}) copy-start(f32[4,12,32,64]{3,2,1,0:T(8,128)S(1)} %fusion.81) | copy-start | bytes 1179652
  209.8 4.2 copy-start.54
  214.0 4.4 copy-start.34
  214.0 4.4 copy-start.35
  214.0 13.6 %slice-start = ((s8[4718592]{0:T(1024)(128)(4,1)}), s8[4194304]{0:T(1024)(128)(4,1)S(1)}, s32[]{:S(2)}) async-start(s8[4718592]{0:T(1024)(128)(4,1)} %bitcast.188), calls=%async_computation | async-start | bytes 8388608
  219.6 8.1 %slice-start.1 = ((s8[4718592]{0:T(1024)(128)(4,1)}), s8[524288]{0:T(1024)(128)(4,1)S(1)}, s32[]{:S(2)}) async-start(s8[4718592]{0:T(1024)(128)(4,1)} %bitcast.188), calls=%async_computation.1 | async-start | bytes 1048576
  219.6 8.1 %copy-start.55 = (f32[768]{0:T(1024)S(1)}, f32[768]{0:T(1024)}, u32[]{:S(2)}) copy-start(f32[768]{0:T(1024)} %convert_reduce_fusion.7) | copy-start | bytes 9220
  227.6 10.2 %copy-start.27 = (bf16[808,768]{1,0:T(8,128)(2,1)S(1)}, bf16[808,768]{1,0:T(8,128)(2,1)}, u32[]{:S(2)}) copy-start(bf16[808,768]{1,0:T(8,128)(2,1)} %convert_element_type.376) | copy-start | bytes 3723268
  237.8 12.3 %copy-start.1 = (f32[808,768]{1,0:T(8,128)S(1)}, f32[808,768]{1,0:T(8,128)}, u32[]{:S(2)}) copy-start(f32[808,768]{1,0:T(8,128)} %reshape.551) | copy-start | bytes 7446532
  291.4 4.2 copy-start.22
  297.8 3.9 copy-start.41
  309.0 5.0 %copy-start.43 = (pred[4,202,12,32]{1,3,2,0:T(32,128)(4,1)S(1)}, pred[4,202,12,32]{1,3,2,0:T(32,128)(4,1)}, u32[]{:S(2)}) copy-start(pred[4,202,12,32]{1,3,2,0:T(32,128)(4,1)} %and_convert_fusion) | copy-start | bytes 930820
  328.1 4.3 copy-start.10
  339.0 4.4 copy-start.24
  339.0 4.4 copy-start.31
  351.7 3.9 copy-start.29
  (34 other events, 71.9 us)

commit v2 on v1

v2 whole, which is shorter than its diff:
```python
import jax
import jax.numpy as jnp
import numpy as np
from jax import lax
from jax.experimental import pallas as pl
from jax.experimental.pallas import tpu as pltpu
from jax.sharding import PartitionSpec as P


MESH = pl.DeviceIdType.MESH
RING = 4
BLK = 48
WID = 768
HALF = 384
ALL = pl.ds(0, RING)


def rounded(value):
    return value.astype(jnp.bfloat16)


def wide(value):
    return value.astype(jnp.float32)


class Net:
    def __init__(self, send_sems, recv_sems):
        self.marks = {}
        self.send_sems, self.recv_sems, self.count, self.open = send_sems, recv_sems, 0, []
        index = lax.axis_index("fsdp")
        self.x = lax.axis_index("dp")
        self.y = index // (2 * RING)
        self.z = (index // 2) % RING
        self.c = index % 2

    def at(self, y, z, c):
        return {"fsdp": ((y + RING) % RING) * (2 * RING) + ((z + RING) % RING) * 2 + c}

    def sibling(self):
        return self.at(self.y, self.z, 1 - self.c)

    def along(self, axis, step):
        if axis == "y":
            return self.at(self.y + step, self.z, self.c)
        if axis == "z":
            return self.at(self.y, self.z + step, self.c)
        return {"dp": (self.x + step) % RING}

    def greet(self):
        barrier = pltpu.get_barrier_semaphore()
        peers = [self.sibling()] + [
            self.along(axis, step) for axis in ("x", "y", "z") for step in (1, 2, 3)
        ]
        for peer in peers:
            pl.semaphore_signal(barrier, inc=1, device_id=peer, device_id_type=MESH)
        pl.semaphore_wait(barrier, len(peers))

    def send(self, src, dst, device):
        slot = self.count
        self.count += 1
        copy = pltpu.make_async_remote_copy(
            src_ref=src,
            dst_ref=dst,
            send_sem=self.send_sems.at[slot],
            recv_sem=self.recv_sems.at[slot],
            device_id=device,
            device_id_type=MESH,
        )
        copy.start()
        self.open.append(copy)
        return slot

    def arrived(self, slot, land):
        pltpu.make_async_remote_copy(
            src_ref=land,
            dst_ref=land,
            send_sem=self.send_sems.at[slot],
            recv_sem=self.recv_sems.at[slot],
            device_id=self.sibling(),
            device_id_type=MESH,
        ).wait_recv()

    def settle(self):
        for copy in self.open:
            copy.wait_send()
        self.open = []

    def partners(self):
        near = [self.along(axis, step) for axis in ("y", "z") for step in (1, -1)]
        return [self.sibling()] + near + [self.along("x", step) for step in (1, 2, 3)]

    def axes(self, way):
        return ("y", "z") if way == 0 else ("z", "y")

    def place(self, way):
        return (self.y, self.z) if way == 0 else (self.z, self.y)


def wrap(index):
    return (index + RING) % RING


def base_of(ref, part):
    return 4 * part if ref.shape[0] == 12 else 4 * (part % 2)


def slot_of(ref, part, way, core, first, second):
    y, z = (first, second) if way == 0 else (second, first)
    piece = 2 * core + way
    base = base_of(ref, part)
    if part < 2:
        return ref.at[base + piece, y, z]
    if not isinstance(y, pl.Slice):
        return ref.at[base + y, z, piece]
    return ref.at[pl.ds(base, RING), z, piece]


def half(ref, side):
    lead = (slice(None),) * (len(ref.shape) - 1)
    return ref.at[lead + (pl.ds(side * HALF, HALF),)]


def gather_steps(net, weights, part):
    ways = (0, 1)
    sent = {}

    def slot(way, first, second, core=None):
        return slot_of(weights, part, way, net.c if core is None else core, first, second)

    for way in ways:
        p, q = net.place(way)
        axis = net.axes(way)[0]
        own = slot(way, p, q)
        sent[way, "r"] = net.send(own, own, net.along(axis, 1))
        sent[way, "l"] = net.send(own, own, net.along(axis, -1))
    yield
    for way in ways:
        p, q = net.place(way)
        axis = net.axes(way)[0]
        left = slot(way, wrap(p - 1), q)
        net.arrived(sent[way, "r"], left)
        sent[way, "fr"] = net.send(half(left, 0), half(left, 0), net.along(axis, 1))
        right = slot(way, wrap(p + 1), q)
        net.arrived(sent[way, "l"], right)
        sent[way, "fl"] = net.send(half(right, 1), half(right, 1), net.along(axis, -1))
    yield
    for way in ways:
        p, q = net.place(way)
        axis = net.axes(way)[1]
        far = slot(way, wrap(p + 2), q)
        net.arrived(sent[way, "fr"], half(far, 0))
        net.arrived(sent[way, "fl"], half(far, 1))
        row = slot(way, ALL, q)
        sent[way, "r2"] = net.send(row, row, net.along(axis, 1))
        sent[way, "l2"] = net.send(row, row, net.along(axis, -1))
        sent[way, "s0"] = net.send(row, row, net.sibling())
    yield
    for way in ways:
        p, q = net.place(way)
        axis = net.axes(way)[1]
        left = slot(way, ALL, wrap(q - 1))
        net.arrived(sent[way, "r2"], left)
        sent[way, "fr2"] = net.send(half(left, 0), half(left, 0), net.along(axis, 1))
        sent[way, "s1"] = net.send(left, left, net.sibling())
        right = slot(way, ALL, wrap(q + 1))
        net.arrived(sent[way, "l2"], right)
        sent[way, "fl2"] = net.send(half(right, 1), half(right, 1), net.along(axis, -1))
        sent[way, "s2"] = net.send(right, right, net.sibling())
    yield
    for way in ways:
        p, q = net.place(way)
        far = slot(way, ALL, wrap(q + 2))
        net.arrived(sent[way, "fr2"], half(far, 0))
        net.arrived(sent[way, "fl2"], half(far, 1))
        sent[way, "s3"] = net.send(far, far, net.sibling())
    yield
    for way in ways:
        p, q = net.place(way)
        other = 1 - net.c
        for name, step in (("s0", 0), ("s1", -1), ("s2", 1), ("s3", 2)):
            net.arrived(sent[way, name], slot(way, ALL, wrap(q + step), other))


def gather_small(net, small):
    own = small.at[net.y, net.z]
    sent = [net.send(own, own, net.along("y", step)) for step in (1, 2, 3)]
    yield
    for slot, step in zip(sent, (1, 2, 3)):
        net.arrived(slot, small.at[wrap(net.y - step), net.z])
    row = small.at[ALL, net.z]
    sent = [net.send(row, row, net.along("z", step)) for step in (1, 2, 3)]
    yield
    for slot, step in zip(sent, (1, 2, 3)):
        net.arrived(slot, small.at[ALL, wrap(net.z - step)])


def load_shards(net, weights, small, stage, small_mine, shards):
    queries, keys, values, outs, ups, downs, packed = shards
    first = net.c == 0

    def rows(slot, core):
        return pl.ds(pl.multiple_of(BLK * slot + 24 * core, 8), 24)

    def lane(piece):
        return pl.ds(pl.multiple_of(WID * piece, WID), WID)

    def exchange(slot, mine, theirs):
        outgoing = pl.ds(4 * BLK + 24 * slot, 24)
        stage[rows(slot, net.c)] = mine
        stage[outgoing] = theirs
        return net.send(stage.at[outgoing], stage.at[rows(slot, net.c)], net.sibling())

    source, target = iota((24, HALF), 1), iota((24, HALF), 0)
    spread = jnp.broadcast_to(wide(packed[...]), (24, HALF)) * flag(source % 24 == target)
    pick = rounded(flag(iota((HALF, 128), 0) // 24 == iota((HALF, 128), 1)))
    small_mine[rows(0, net.c)] = dot(rounded(spread), pick)
    sent_small = net.send(small_mine.at[rows(0, net.c)], small_mine.at[rows(0, net.c)], net.sibling())
    sent = []
    for way in (0, 1):
        early, late = ((queries, values), (keys, outs))[way]
        early, late = wide(early[...]), wide(late[...])
        sent.append(exchange(way, jnp.where(first, early, late), jnp.where(first, late, early)))
    for way in (0, 1):
        near, away = 2 * net.c + way, 2 - 2 * net.c + way
        sent.append(exchange(2 + way, wide(ups[:, lane(near)]), wide(ups[:, lane(away)])))
    for way in (0, 1):
        weights[8 + net.y, net.z, 2 * net.c + way] = downs[pl.ds(BLK * way, BLK)]
    yield
    net.arrived(sent_small, small_mine.at[rows(0, 1 - net.c)])
    small[net.y, net.z] = rounded(small_mine[...])
    for slot in (0, 1, 2, 3):
        if slot == 2:
            yield
        net.arrived(sent[slot], stage.at[rows(slot, 1 - net.c)])
        piece = 4 * (slot // 2) + 2 * net.c + slot % 2
        weights[piece, net.y, net.z] = rounded(stage[pl.ds(BLK * slot, BLK)])


def add_blocks(target, source):
    if len(target.shape) == 2:
        target[...] = rounded(wide(target[...]) + wide(source[...]))
        return
    for index in range(target.shape[0]):
        add_blocks(target.at[index], source.at[index])


def add_two(target, one, two):
    if len(target.shape) == 2:
        target[...] = rounded(wide(target[...]) + wide(one[...]) + wide(two[...]))
        return
    for index in range(target.shape[0]):
        add_two(target.at[index], one.at[index], two.at[index])


def ring_reduce(net, group, land, axis, me):
    ahead, behind, far = wrap(me + 1), wrap(me - 1), wrap(me + 2)
    right, left = net.along(axis, 1), net.along(axis, -1)
    one_r = net.send(half(group(far), 0), land.at[0], right)
    one_l = net.send(half(group(far), 1), land.at[1], left)
    two_r = net.send(half(group(ahead), 1), land.at[2], right)
    two_l = net.send(half(group(behind), 0), land.at[3], left)
    yield
    net.arrived(one_r, land.at[0])
    add_blocks(half(group(ahead), 0), land.at[0])
    three_r = net.send(half(group(ahead), 0), land.at[4], right)
    net.arrived(one_l, land.at[1])
    add_blocks(half(group(behind), 1), land.at[1])
    three_l = net.send(half(group(behind), 1), land.at[5], left)
    yield
    net.arrived(two_r, land.at[2])
    net.arrived(three_l, land.at[5])
    add_two(half(group(me), 1), land.at[2], land.at[5])
    net.arrived(two_l, land.at[3])
    net.arrived(three_r, land.at[4])
    add_two(half(group(me), 0), land.at[3], land.at[4])


def together(*steps):
    steps = list(steps)
    while steps:
        steps = [step for step in steps if next(step, steps) is not steps]
        if steps:
            yield


def strip(result, part, piece):
    if part == 0:
        return result.at[piece]
    return result.at[:, pl.ds(pl.multiple_of(WID * piece, WID), WID)]


def reduce_steps(net, grads, part, pair, pair_credit, big, little, cross, total, result):
    ways = (0, 1)

    def slot(way, first, second):
        return slot_of(grads, part, way, net.c, first, second)

    def whole(way, core):
        if part < 2:
            return grads.at[base_of(grads, part) + 2 * core + way]
        return grads.at[pl.ds(base_of(grads, part), RING), ALL, 2 * core + way]

    if part != 2:
        pl.semaphore_wait(pair_credit, 1)
    sent = [net.send(whole(way, 1 - net.c), pair.at[way], net.sibling()) for way in ways]
    yield
    for way in ways:
        net.arrived(sent[way], pair.at[way])
        for index in range(RING):
            add_blocks(whole(way, net.c).at[index], pair.at[way, index])
    if part != 0:
        pl.semaphore_signal(pair_credit, inc=1, device_id=net.sibling(), device_id_type=MESH)
    yield from together(
        *[
            ring_reduce(
                net,
                lambda at, way=way: slot(way, ALL, at),
                big.at[way],
                net.axes(way)[1],
                net.place(way)[1],
            )
            for way in ways
        ]
    )
    yield
    yield from together(
        *[
            ring_reduce(
                net,
                lambda at, way=way: slot(way, at, net.place(way)[1]),
                little.at[way],
                net.axes(way)[0],
                net.place(way)[0],
            )
            for way in ways
        ]
    )
    sent = {}
    for way in ways:
        cross[way, net.x] = slot(way, *net.place(way))[...]
        for step in (1, 2, 3):
            mine = cross.at[way, net.x]
            sent[way, step] = net.send(mine, mine, net.along("x", step))
    yield
    for way in ways:
        for step in (1, 2, 3):
            net.arrived(sent[way, step], cross.at[way, wrap(net.x - step)])
        target = result.at[pl.ds(BLK * way, BLK)] if part == 2 else total.at[way]
        target[...] = (
            (wide(cross[way, 0]) + wide(cross[way, 1])) + wide(cross[way, 2])
        ) + wide(cross[way, 3])
    if part == 2:
        return
    sent = []
    for way in ways:
        mine = strip(result, part, 2 * net.c + way)
        mine[...] = total[way, pl.ds(pl.multiple_of(24 * net.c, 8), 24)]
        sent.append(
            net.send(
                total.at[way, pl.ds(pl.multiple_of(24 - 24 * net.c, 8), 24)], mine, net.sibling()
            )
        )
    yield
    for way in ways:
        net.arrived(sent[way], strip(result, part, 2 - 2 * net.c + way))


def vector_steps(net, vectors, land):
    sent = net.send(vectors, land.at[0, 0], net.sibling())
    yield
    net.arrived(sent, land.at[0, 0])
    value = vectors[...] + land[0, 0]
    for stage, axis, me in ((1, "z", net.z), (2, "y", net.y), (3, "x", net.x)):
        land[stage, me] = value
        mine = land.at[stage, me]
        sent = [net.send(mine, mine, net.along(axis, step)) for step in (1, 2, 3)]
        yield
        for step in (1, 2, 3):
            net.arrived(sent[step - 1], land.at[stage, wrap(me - step)])
        value = ((land[stage, 0] + land[stage, 1]) + land[stage, 2]) + land[stage, 3]
    land[0, 1] = value

ROWS = 202
PAD = 208
MOLS = 4
TOTAL = MOLS * PAD
GROUPS = 3
LANES = 256
FEAT = 128
EPS_NORM = 1e-05
EPS_ATTN = 1e-06
GELU_SCALE = 0.7978845608028654
GELU_CUBIC = 0.044715


def dot(left, right):
    return jnp.dot(left, right, preferred_element_type=jnp.float32)


def dot_nt(left, right):
    return lax.dot_general(left, right, (((1,), (1,)), ((), ())), preferred_element_type=jnp.float32)


def dot_tn(left, right):
    return lax.dot_general(left, right, (((0,), (0,)), ((), ())), preferred_element_type=jnp.float32)


def square(ref, index):
    return ref[index].reshape(WID, WID)


def iota(shape, axis):
    return lax.broadcasted_iota(jnp.int32, shape, axis)


def flag(condition):
    return jnp.where(condition, 1.0, 0.0)


def softplus(value):
    small = jnp.exp(-jnp.abs(value))
    tail = jnp.where(small < 1e-3, small * (1.0 - 0.5 * small), jnp.log(1.0 + small))
    return jnp.maximum(value, 0.0) + tail


def softplus_slope(feature):
    return jnp.where(feature < 1e-3, feature * (1.0 - 0.5 * feature), 1.0 - jnp.exp(-feature))


def centred(value):
    centre = value - jnp.mean(value, axis=-1, keepdims=True)
    scale = lax.rsqrt(jnp.mean(centre * centre, axis=-1, keepdims=True) + EPS_NORM)
    return centre * scale, scale


def rows_of(molecule):
    return pl.ds(pl.multiple_of(molecule * PAD, 16), PAD)


def column_sum(value):
    return jnp.sum(value, axis=0, keepdims=True)


GAIN1, BIAS1, B_QUERY, B_KEY, B_VALUE, B_OUT, GAIN2, BIAS2, B_DOWN, B_UP = range(10)


class Layer:
    def __init__(self, **refs):
        self.__dict__.update(refs)

    def row(self, index):
        return self.params[pl.ds(index, 1)]

    def add_row(self, index, value):
        self.vectors[pl.ds(index, 1)] += value

    def block_mask(self):
        shape = (FEAT, LANES)
        return flag(iota(shape, 0) // 32 == iota(shape, 1) // 64)

    def prepare_features(self):
        proj = self.feature_ref[...]
        pick_rows = iota((LANES, 64), 0) % 64
        swap = iota((LANES, 64), 1)
        same = rounded(flag(pick_rows == swap))
        turned = rounded(flag(pick_rows + 32 == swap) - flag(pick_rows == swap + 32))
        spread = rounded(flag(iota((32, FEAT), 1) % 32 == iota((32, FEAT), 0)))
        mask = flag(iota((LANES, FEAT), 0) // 64 == iota((LANES, FEAT), 1) // 32)
        for index, pick in ((0, same), (1, turned)):
            tall = rounded(dot(pick, proj))
            self.features[index] = rounded(dot(tall, spread) * mask)

    def prepare_tokens(self):
        zero = jnp.zeros((16, WID), jnp.bfloat16)
        for molecule in range(MOLS):
            start = molecule * PAD
            self.tokens[pl.ds(start + PAD - 16, 16)] = zero
            self.tokens[pl.ds(start, ROWS)] = self.raw[molecule]

    def prepare_cotangent(self):
        most = jnp.maximum(
            jnp.maximum(self.lengths[0], self.lengths[1]), jnp.maximum(self.lengths[2], self.lengths[3])
        )
        zero = jnp.zeros((16, WID), jnp.bfloat16)
        keep = iota((ROWS, WID), 0) < most
        for molecule in range(MOLS):
            start = molecule * PAD
            self.grad_down[pl.ds(start + PAD - 16, 16)] = zero
            masked = jnp.where(keep, wide(self.raw[molecule]), 0.0)
            self.grad_down[pl.ds(start, ROWS)] = rounded(masked)
            self.add_row(B_DOWN, column_sum(masked))

    def prepare_params(self):
        columns = wide(self.small[...].reshape(WID, 128))
        rows = columns.T
        self.params[pl.ds(0, 16)] = rows[0:16]
        lanes = iota((8, WID), 1)
        owner = flag(lanes // 192 == iota((8, WID), 0))
        stacked = jnp.concatenate(
            [jnp.broadcast_to(rows[B_UP + k : B_UP + k + 1], (8, WID)) * owner for k in range(4)], axis=0
        )
        source = iota((WID, WID), 0)
        pick = rounded(flag(96 * ((source // 24) % 8) + source % 24 == iota((WID, WID), 1)))
        spread = dot(rounded(stacked), pick)
        total = spread[0:8]
        for k in range(1, 4):
            total = total + pltpu.roll(spread[8 * k : 8 * k + 8], 24 * k, 1)
        self.params[pl.ds(16, 8)] = total

    def norm_one(self):
        gain, bias = self.row(GAIN1), self.row(BIAS1)
        for molecule in range(MOLS):
            rows = pl.ds(molecule * PAD, PAD)
            normed, _ = centred(wide(self.tokens[rows]))
            self.normed_one[rows] = rounded(normed * gain + bias)

    def turn(self, value, group):
        both = value[:, group * LANES : (group + 1) * LANES]
        cosines = jnp.concatenate([self.cosines[...]] * 2, axis=1)
        sines = jnp.concatenate([self.sines[...]] * 2, axis=1)
        return rounded(both * cosines), rounded(both * sines)

    def state(self, molecule, group, mask):
        rows, ones = rows_of(molecule), jnp.ones((PAD, LANES), jnp.bfloat16)
        keys = self.feat_key[rows, group * FEAT : (group + 1) * FEAT]
        values = self.values[rows, group * LANES : (group + 1) * LANES]
        return jnp.concatenate(
            [rounded(dot_tn(keys, values) * mask), rounded(dot_tn(keys, ones) * mask)], axis=1
        )

    def attend(self, molecule):
        rows = rows_of(molecule)
        normed = self.normed_one[rows]
        query = dot(normed, square(self.weights, 0)) + self.row(B_QUERY)
        key = dot(normed, square(self.weights, 1)) + self.row(B_KEY)
        value = dot(normed, square(self.weights, 2)) + self.row(B_VALUE)
        length = self.lengths[molecule]
        valid = jnp.where(iota((PAD, WID), 0) < length, value, 0.0)
        level = column_sum(valid) / wide(jnp.maximum(length, 1))
        self.levels[pl.ds(8 * molecule, 1)] = level
        self.values[rows] = rounded(value - level)
        keep = iota((PAD, FEAT), 0) < length
        mask = self.block_mask()
        for group in range(GROUPS):
            lanes = slice(group * FEAT, (group + 1) * FEAT)
            cos_part, sin_part = self.turn(query, group)
            feat = softplus(dot(cos_part, self.features[0]) + dot(sin_part, self.features[1]))
            feat_query = rounded(feat)
            self.feat_query[rows, lanes] = feat_query
            cos_part, sin_part = self.turn(key, group)
            feat = softplus(dot(cos_part, self.features[0]) + dot(sin_part, self.features[1]))
            self.feat_key[rows, lanes] = rounded(jnp.where(keep, feat, 0.0))
            state = self.state(molecule, group, mask)
            self.states[molecule, group] = state
            both = dot(feat_query, state)
            centre = level[:, group * LANES : (group + 1) * LANES]
            mixed = centre + (both[:, :LANES] - EPS_ATTN * centre) / (both[:, LANES:] + EPS_ATTN)
            self.mixed[rows, group * LANES : (group + 1) * LANES] = rounded(mixed)

    def middle_rows(self, molecule):
        rows = rows_of(molecule)
        middle = (
            wide(self.tokens[rows])
            + dot(self.mixed[rows], square(self.weights, 3))
            + self.row(B_OUT)
        )
        self.middle[rows] = middle
        normed, _ = centred(middle)
        self.normed_two[rows] = rounded(normed * self.row(GAIN2) + self.row(BIAS2))

    def up_rows(self, quarter, molecule):
        rows = rows_of(molecule)
        pre = dot(self.normed_two[rows], square(self.weights, 4 + quarter)) + self.row(16 + quarter)
        squared = pre * pre
        gate = 0.5 + 0.5 * jnp.tanh(pre * (GELU_SCALE + GELU_SCALE * GELU_CUBIC * squared))
        hidden = pre * gate
        slope = gate + (hidden - hidden * gate) * (
            2.0 * GELU_SCALE + 6.0 * GELU_SCALE * GELU_CUBIC * squared
        )
        self.hidden[quarter, rows] = rounded(hidden)
        self.slope[quarter, rows] = rounded(slope)

    def store_term(self, slot, value):
        self.grads[slot] = rounded(value).reshape(4, 4, BLK, WID)

    def term_down(self, quarter):
        self.store_term(quarter, dot_tn(self.hidden[quarter], self.grad_down[...]))

    def grad_pre_rows(self, quarter, molecule):
        rows = rows_of(molecule)
        grad_hidden = dot_nt(self.grad_down[rows], square(self.weights, 8 + quarter))
        grad_pre = rounded(grad_hidden * wide(self.slope[quarter, rows]))
        self.slope[quarter, rows] = grad_pre
        self.add_row(B_UP + quarter, column_sum(wide(grad_pre)))

    def term_up(self, quarter):
        self.store_term(4 + quarter, dot_tn(self.normed_two[...], self.slope[quarter]))

    def grad_middle_rows(self, molecule):
        rows = rows_of(molecule)
        grad_two = dot_nt(self.slope[0, rows], square(self.weights, 4))
        for quarter in range(1, 4):
            grad_two += dot_nt(self.slope[quarter, rows], square(self.weights, 4 + quarter))
        normed, scale = centred(self.middle[rows])
        self.add_row(GAIN2, column_sum(grad_two * normed))
        self.add_row(BIAS2, column_sum(grad_two))
        scaled = grad_two * self.row(GAIN2)
        first = jnp.mean(scaled, axis=-1, keepdims=True)
        second = jnp.mean(scaled * normed, axis=-1, keepdims=True)
        self.grad_middle[rows] = wide(self.grad_down[rows]) + scale * (scaled - first - normed * second)

    def branch_rows(self, molecule):
        rows = rows_of(molecule)
        low = rounded(self.grad_middle[rows])
        self.slope[3, rows] = low
        self.add_row(B_OUT, column_sum(wide(low)))

    def term_out(self):
        self.store_term(3, dot_tn(self.mixed[...], self.slope[3]))

    def attend_back(self, molecule):
        rows = rows_of(molecule)
        grad_mixed = dot_nt(self.slope[3, rows], square(self.weights, 3))
        mask = self.block_mask()
        both_mask = jnp.concatenate([mask, mask], axis=1)
        ones = jnp.ones((PAD, LANES), jnp.bfloat16)
        cosines = jnp.concatenate([self.cosines[...]] * 2, axis=1)
        sines = jnp.concatenate([self.sines[...]] * 2, axis=1)
        for group in range(GROUPS):
            thin = slice(group * FEAT, (group + 1) * FEAT)
            lanes = slice(group * LANES, (group + 1) * LANES)
            feat_query, feat_key = self.feat_query[rows, thin], self.feat_key[rows, thin]
            values, state = self.values[rows, lanes], self.states[molecule, group]
            both = dot(feat_query, state)
            inverse = 1.0 / (both[:, LANES:] + EPS_ATTN)
            grad_num = grad_mixed[:, lanes] * inverse
            offset = EPS_ATTN * self.levels[pl.ds(8 * molecule, 1), lanes]
            grad_den = -grad_num * ((both[:, :LANES] - offset) * inverse)
            grad_both = jnp.concatenate([rounded(grad_num), rounded(grad_den)], axis=1)
            grad_feat_query = dot_nt(grad_both, state)
            grad_state = rounded(dot_tn(feat_query, grad_both) * both_mask)
            grad_feat_key = dot_nt(jnp.concatenate([values, ones], axis=1), grad_state)
            grad_value = rounded(dot(feat_key, grad_state[:, :LANES]))
            self.slope[2, rows, lanes] = grad_value
            self.add_lanes(B_VALUE, group, grad_value)
            for slot, row, feat, grad in (
                (0, B_QUERY, feat_query, grad_feat_query),
                (1, B_KEY, feat_key, grad_feat_key),
            ):
                grad = rounded(grad * softplus_slope(wide(feat)))
                low = rounded(
                    cosines * dot_nt(grad, self.features[0]) + sines * dot_nt(grad, self.features[1])
                )
                self.slope[slot, rows, lanes] = low
                self.add_lanes(row, group, low)

    def add_lanes(self, row, group, value):
        self.vectors[pl.ds(row, 1), group * LANES : (group + 1) * LANES] += column_sum(wide(value))

    def term_square(self, index):
        self.store_term(index, dot_tn(self.normed_one[...], self.slope[index]))

    def grad_token_rows(self, molecule):
        rows = rows_of(molecule)
        grad_one = dot_nt(self.slope[0, rows], square(self.weights, 0))
        for index in (1, 2):
            grad_one += dot_nt(self.slope[index, rows], square(self.weights, index))
        normed, scale = centred(wide(self.tokens[rows]))
        self.add_row(GAIN1, column_sum(grad_one * normed))
        self.add_row(BIAS1, column_sum(grad_one))
        scaled = grad_one * self.row(GAIN1)
        first = jnp.mean(scaled, axis=-1, keepdims=True)
        second = jnp.mean(scaled * normed, axis=-1, keepdims=True)
        grad = self.grad_middle[rows] + scale * (scaled - first - normed * second)
        self.raw[molecule] = rounded(grad[:ROWS])

    def layer_out_rows(self, molecule):
        rows = rows_of(molecule)
        result = self.middle[rows] + self.row(B_DOWN)
        for quarter in range(4):
            result += dot(self.hidden[quarter, rows], square(self.weights, 8 + quarter))
        most = jnp.maximum(
            jnp.maximum(self.lengths[0], self.lengths[1]), jnp.maximum(self.lengths[2], self.lengths[3])
        )
        keep = iota((ROWS, WID), 0) < most
        self.raw[molecule] = rounded(jnp.where(keep, result[:ROWS], 0.0))


def each(work):
    def step(molecule, carry):
        work(molecule)
        return carry

    lax.fori_loop(0, MOLS, step, 0)


LAYER_SCRATCH = dict(
    raw=((MOLS, ROWS, WID), jnp.bfloat16),
    tokens=((TOTAL, WID), jnp.bfloat16),
    grad_down=((TOTAL, WID), jnp.bfloat16),
    normed_one=((TOTAL, WID), jnp.bfloat16),
    values=((TOTAL, WID), jnp.bfloat16),
    mixed=((TOTAL, WID), jnp.bfloat16),
    normed_two=((TOTAL, WID), jnp.bfloat16),
    feat_query=((TOTAL, HALF), jnp.bfloat16),
    feat_key=((TOTAL, HALF), jnp.bfloat16),
    levels=((8 * MOLS, WID), jnp.float32),
    states=((MOLS, GROUPS, FEAT, 2 * LANES), jnp.bfloat16),
    middle=((TOTAL, WID), jnp.float32),
    grad_middle=((TOTAL, WID), jnp.float32),
    hidden=((4, TOTAL, WID), jnp.bfloat16),
    slope=((4, TOTAL, WID), jnp.bfloat16),
    features=((2, LANES, FEAT), jnp.bfloat16),
    params=((24, WID), jnp.float32),
    vectors=((16, WID), jnp.float32),
    grads=((8, 4, 4, BLK, WID), jnp.bfloat16),
    weights=((12, 4, 4, BLK, WID), jnp.bfloat16),
    small=((4, 4, BLK, 128), jnp.bfloat16),
)


VMEM = pl.BlockSpec(memory_space=pltpu.VMEM)
SMEM = pl.BlockSpec(memory_space=pltpu.SMEM)
ANY = pl.BlockSpec(memory_space=pl.ANY)
SEMS = 224


def landing(name):
    bf = jnp.bfloat16
    return {
        name + "_big": ((2, 6, 4, BLK, HALF), bf),
        name + "_little": ((2, 6, BLK, HALF), bf),
        name + "_cross": ((2, 4, BLK, WID), bf),
    }


COMM_SCRATCH = dict(
    pair=((2, 4, 4, BLK, WID), jnp.bfloat16),
    **landing("odd"),
    **landing("even"),
    total_zero=((2, BLK, WID), jnp.float32),
    total_one=((2, BLK, WID), jnp.float32),
    square_sum=((4, 24, WID), jnp.float32),
    up_sum=((24, 4 * WID), jnp.float32),
    down_sum=((2 * BLK, WID), jnp.float32),
    vector_land=((4, 4, 16, WID), jnp.float32),
    narrow=((16, 128), jnp.float32),
    small_mine=((BLK, 128), jnp.float32),
)
LOADS = ("tokens", "cotangent")
OUTS = ("layer", "tokens", "square", "up", "down", "narrow")


def some(work, *molecules):
    def step(molecule, carry):
        work(molecule)
        return carry

    lax.fori_loop(molecules[0], molecules[-1] + 1, step, 0)


def layer_kernel(
    lengths, queries, keys, values, outs, ups, downs, packed, feature_ref, cosines, sines,
    tokens_in, cot_in, layer_out, tokens_out, square_out, up_out, down_out, narrow_out, *scratch,
):
    names = list(LAYER_SCRATCH) + list(COMM_SCRATCH)
    refs = dict(zip(names, scratch))
    send_sems, recv_sems, local_sems, credits, pair_credit = scratch[len(names):]
    net = Net(send_sems, recv_sems)
    work = Layer(
        lengths=lengths, feature_ref=feature_ref, cosines=cosines, sines=sines,
        **{name: refs[name] for name in LAYER_SCRATCH},
    )
    load_tokens = pltpu.make_async_copy(tokens_in, work.raw, local_sems.at[0])
    load_cot = pltpu.make_async_copy(cot_in, work.raw, local_sems.at[1])
    load_tokens.start()
    net.greet()

    shards = (queries, keys, values, outs, ups, downs, packed)
    load = load_shards(
        net, work.weights, work.small, work.grad_middle, refs["small_mine"], shards
    )
    small = gather_small(net, work.small)
    get = [gather_steps(net, work.weights, part) for part in (0, 1, 2)]

    def go(*steps):
        for step in steps:
            next(step, None)

    go(load)
    work.vectors[...] = jnp.zeros_like(work.vectors)
    work.prepare_features()
    go(load, small, get[0], load, get[1])
    load_tokens.wait()
    work.prepare_tokens()
    load_cot.start()
    go(get[0], small, get[0], get[1])
    load_cot.wait()
    work.prepare_cotangent()
    go(small)
    work.prepare_params()
    go(get[0], get[1])
    work.norm_one()
    go(get[0], get[2], get[0], get[2])
    some(work.attend, 0, 1)
    go(get[1], get[2])
    some(work.attend, 2, 3)
    some(work.middle_rows, 0, 3)
    go(get[1], get[1], get[2])
    for quarter in range(4):
        some(lambda molecule: work.up_rows(quarter, molecule), 0, 3)
        if quarter == 0:
            go(get[2])
    for quarter in range(4):
        work.term_down(quarter)
    go(get[2])
    net.settle()

    def reduce(part, name, total, result):
        return reduce_steps(
            net, work.grads, part, refs["pair"], pair_credit, refs[name + "_big"], refs[name + "_little"],
            refs[name + "_cross"], total, refs[result],
        )

    down = reduce(2, "even", None, "down_sum")
    up = reduce(1, "odd", refs["total_one"], "up_sum")
    squares = reduce(0, "even", refs["total_zero"], "square_sum")
    go(down)
    for quarter in range(4):
        some(lambda molecule: work.grad_pre_rows(quarter, molecule), 0, 3)
        go(*[down] * (quarter % 2))
    for quarter in range(4):
        work.term_up(quarter)
        go(*[down] * (quarter % 2))
    go(up)
    some(work.grad_middle_rows, 0, 1)
    go(down)
    some(work.grad_middle_rows, 2, 3)
    some(work.branch_rows, 0, 3)
    go(down, up, down)
    some(work.attend_back, 0, 0)
    go(up, down)
    some(work.attend_back, 1, 1)
    go(up, down)
    some(work.attend_back, 2, 2)
    go(up, down)
    some(work.attend_back, 3, 3)
    for _ in down:
        pass
    net.settle()
    for device in net.partners():
        pl.semaphore_signal(credits, inc=1, device_id=device, device_id_type=MESH)
    for index in range(3):
        work.term_square(index)
    work.term_out()
    pl.semaphore_wait(credits, 8)
    go(squares, up)
    some(work.grad_token_rows, 0, 3)
    write_tokens = pltpu.make_async_copy(work.raw, tokens_out, local_sems.at[0])
    write_tokens.start()
    vectors = vector_steps(net, work.vectors, refs["vector_land"])
    go(squares, vectors, up)
    write_tokens.wait()
    some(work.layer_out_rows, 0, 1)
    go(squares, vectors, up)
    some(work.layer_out_rows, 2, 3)
    write_layer = pltpu.make_async_copy(work.raw, layer_out, local_sems.at[1])
    write_layer.start()
    for _ in together(squares, vectors, up):
        pass
    total = refs["vector_land"][0, 1]
    place = net.y * 8 + net.z * 2 + net.c
    narrow = refs["narrow"]
    turned = pltpu.roll(total, WID - 24 * place, 1)
    narrow[...] = turned[:, :128]
    chosen = refs["vector_land"][0, 1, pl.ds(B_UP + place // 8, 1)]
    narrow[pl.ds(B_UP, 1)] = pltpu.roll(chosen, WID - 96 * (place % 8), 1)[:, :128]
    writes = [
        pltpu.make_async_copy(refs[name], ref, local_sems.at[2 + slot])
        for slot, (name, ref) in enumerate(
            (("square_sum", square_out), ("up_sum", up_out), ("down_sum", down_out), ("narrow", narrow_out))
        )
    ]
    for write in writes:
        write.start()
    net.settle()
    for write in [write_layer] + writes:
        write.wait()


def layer_call(*operands):
    bf, ff = jnp.bfloat16, jnp.float32
    scratch = list(LAYER_SCRATCH.values()) + list(COMM_SCRATCH.values())
    return pl.pallas_call(
        layer_kernel,
        out_shape=(
            jax.ShapeDtypeStruct((MOLS, ROWS, WID), bf),
            jax.ShapeDtypeStruct((MOLS, ROWS, WID), bf),
            jax.ShapeDtypeStruct((4, 24, WID), ff),
            jax.ShapeDtypeStruct((24, 4 * WID), ff),
            jax.ShapeDtypeStruct((2 * BLK, WID), ff),
            jax.ShapeDtypeStruct((16, 128), ff),
        ),
        in_specs=[SMEM] + [VMEM] * 10 + [ANY] * 2,
        out_specs=(ANY,) * 6,
        scratch_shapes=[pltpu.VMEM(shape, dtype) for shape, dtype in scratch]
        + [
            pltpu.SemaphoreType.DMA((SEMS,)),
            pltpu.SemaphoreType.DMA((SEMS,)),
            pltpu.SemaphoreType.DMA((6,)),
            pltpu.SemaphoreType.REGULAR,
            pltpu.SemaphoreType.REGULAR,
        ],
        compiler_params=pltpu.CompilerParams(
            collective_id=0, has_side_effects=True, vmem_limit_bytes=64 * 2**20 - 2**17
        ),
    )(*operands)


def angle_tables():
    positions = np.arange(PAD)[:, None]
    angles = positions * 10000.0 ** (-2.0 * (np.arange(128)[None, :] % 32) / 64)
    return np.cos(angles).astype(np.float32), np.sin(angles).astype(np.float32)


def body(
    tokens, lengths, feature_proj, ln1_gain, ln1_bias, w_query, b_query, w_key, b_key, w_value, b_value,
    w_out, b_out, ln2_gain, ln2_bias, w_up, b_up, w_down, b_down, cotangent,
):
    cosines, sines = angle_tables()
    packed = jnp.concatenate(
        [ln1_gain, ln1_bias, b_query, b_key, b_value, b_out, ln2_gain, ln2_bias, b_down, b_up]
        + [jnp.zeros((HALF - 312,), jnp.bfloat16)]
    ).reshape(1, HALF)
    layer_out, grad_tokens, square, up, down, narrow = layer_call(
        lengths, w_query, w_key, w_value, w_out, w_up, w_down, packed, feature_proj,
        jnp.asarray(cosines), jnp.asarray(sines), tokens, cotangent,
    )
    small = [narrow[index, :24] for index in range(9)]
    return (
        layer_out, grad_tokens, small[0], small[1], square[0], small[2], square[1], small[3], square[2], small[4],
        square[3], small[5], small[6], small[7], up, narrow[9, :96], down, small[8],
    )


def solution(mesh):
    rows, flat = P("fsdp", None), P("fsdp")
    mols = P(("fsdp", "dp"), None, None)
    pairs = (flat, flat, rows, flat, rows, flat, rows, flat, rows, flat, flat, flat, rows, flat, rows, flat)
    return jax.shard_map(
        body,
        mesh=mesh,
        in_specs=(mols, P(("fsdp", "dp")), P()) + pairs + (mols,),
        out_specs=(mols, mols) + pairs,
        check_vma=False,
    )
```

time: 478 us -> 195 us (0.41)
  local copies, waits for them, and re-layouts: 175 us -> 20.5 us
  matrix products: 127 us -> 0 us
  Pallas kernels: 137 us -> 170 us
  other arithmetic: 29.4 us -> 0 us
    dot_general x30 -> x0, matrix products: 127 us -> none  [the longest x6 33.2 us: outer_product(): lax.dot_general(left, right, (((0,), (0,)), ((), ())), preferred_element_...]
    convert_element_type x18 -> x0, local copies, waits for them, and re-layouts: 39.4 us -> none  [the longest x2 8.42 us: body(): value_low = grad_value.astype(jnp.bfloat16)]
    slice x8 -> x0, local copies, waits for them, and re-layouts: 38.2 us -> none  [the longest x2 22.8 us: turned(): high_half = heads_in[..., half_size:]]
    unnamed x141 -> x19, local copies, waits for them, and re-layouts: 48.4 us -> 11.3 us
    pallas_call x2 -> x1, Pallas kernels: 137 us -> 170 us  [layer_call(): pl.pallas_call(layer_kernel, out_shape=(jax.ShapeDtypeStruct((MOLS, ROWS,...]
    reshape x12 -> x1, local copies, waits for them, and re-layouts: 24.7 us -> 0.57 us  [body(): packed = jnp.concatenate([ln1_gain, ln1_bias, b_query, b_key, b_value, b_...]
    reduce_sum x10 -> x0, other arithmetic: 14 us -> none  [the longest x4 5.99 us: column_sums(): return jnp.sum(rows_in.astype(jnp.float32), axis=0)]
    another operation x27 -> x0, local copies, waits for them, and re-layouts: 10.8 us -> none  [the longest x15 8.11 us: body(): jnp.stack([ln1_gain, ln1_bias, b_query, b_key, b_value, b_out, ln2_gain,...]
where the time goes in v2:
time: 195 us; the launch traced here: 192 us
  Pallas kernels  170 us (87%)
  local copies, waits for them, and re-layouts  20.5 us (11%)
    pallas_call x1, Pallas kernels, layer_call(): pl.pallas_call(layer_kernel, out_shape=(jax.ShapeDtypeStruct((MOLS, ROWS,...  170 us
    unnamed x19, local copies, waits for them, and re-layouts  11.3 us
    concatenate x1, local copies, waits for them, and re-layouts, body(): jnp.concatenate([ln1_gain, ln1_bias, b_query, b_key, b_value, b_out, ln2_...  6.87 us

profile of v2, /device:TPU:1, one launch (start us, length us, event | category | flops | bytes accessed | tf_op | source)
XLA Modules:
  0.0 191.7 jit_solution(18210228729169648481)
XLA Ops:
  0.7 0.0 copy-start.1
  0.7 6.9 %concatenate.3 = bf16[384]{0:T(512)(128)(2,1)S(1)} concatenate(bf16[24]{0:T(256)(128)(2,1)} %param.25, bf16[24]{0:T(256)(128)(2,1)} %param.26, bf16[24]{0:T(256)(128)(2,1)} %param.28, bf16[24]{0:T(256)(128)(2,1)} %param.30, bf16[24]{0:T(256)(128)(2,1)} %param.32, bf16[24]{0:T(256)(128)(2,1)} %param.34, bf16[24]{0:T(256)(128)(2,1)} %param.35, bf16[24]{0:T(256)(128)(2,1)} %param.36, ...), dimensions={0} | concatenate | bytes 1536 | tf_op jit(solution)/shard_map/concatenate | solution.py:931
  7.5 0.6 reshape.39.packed
  8.1 1.4 copy.40.feature_ref
  9.5 2.5 %copy.41.tokens_in = bf16[4,202,768]{2,1,0:T(8,128)(2,1)} copy(bf16[4,202,768]{2,0,1:T(4,128)(2,1)} %param.22) | data formatting | bytes 2482176 | tf_op args[0]
  12.0 0.0 copy-done.1
  12.0 1.2 copy.42.cot_in
  13.2 170.2 %shard_map.349 = (bf16[4,202,768]{2,1,0:T(8,128)(2,1)}, bf16[4,202,768]{2,1,0:T(8,128)(2,1)}, f32[4,24,768]{2,1,0:T(8,128)}, f32[24,3072]{1,0:T(8,128)}, f32[96,768]{1,0:T(8,128)}, /*index=5*/f32[16,128]{1,0:T(8,128)}) custom-call(s32[4]{0:T(128)} %lengths.1, bf16[24,768]{1,0:T(8,128)(2,1)} %queries.1, bf16[24,768]{1,0:T(8,128)(2,1)} %keys.1, ...), custom_call_target="tpu_custom_call" | custom-call | tf_op jit(solution)/shard_map/pallas_call | solution.py:894
  183.4 0.0 copy-start.5
  183.4 0.0 copy-start.4
  183.4 0.0 copy-start
  183.4 3.1 %copy.43 = bf16[4,202,768]{2,0,1:T(4,128)(2,1)} copy(bf16[4,202,768]{2,1,0:T(8,128)(2,1)} %get-tuple-element.30) | data formatting | bytes 2482176
  186.5 0.0 copy-done.5
  186.5 0.5 slice_bitcast_fusion.5
  187.0 0.5 slice_bitcast_fusion.4
  187.6 0.0 copy-done.4
  187.6 0.7 slice_bitcast_fusion
  188.3 0.0 copy-start.3
  188.3 0.0 copy-done
  188.3 1.7 copy.44
  190.0 0.0 copy-done.3
  190.0 0.7 copy.47
  190.7 0.0 copy-done.2
  190.7 0.7 copy.48
  (2 shorter events, 0.0 us)
Async XLA Ops:
  0.7 11.3 %copy-start.1 = (bf16[4,202,768]{2,0,1:T(4,128)(2,1)S(1)}, bf16[4,202,768]{2,0,1:T(4,128)(2,1)}, u32[]{:S(2)}) copy-start(bf16[4,202,768]{2,0,1:T(4,128)(2,1)} %param.41) | copy-start | bytes 3723268
  183.4 3.1 %copy-start.5 = (f32[16,128]{1,0:T(8,128)S(1)}, f32[16,128]{1,0:T(8,128)}, u32[]{:S(2)}) copy-start(f32[16,128]{1,0:T(8,128)} %get-tuple-element.26) | copy-start | bytes 24580
  183.4 4.2 %copy-start.4 = (f32[4,24,768]{2,1,0:T(8,128)S(1)}, f32[4,24,768]{2,1,0:T(8,128)}, u32[]{:S(2)}) copy-start(f32[4,24,768]{2,1,0:T(8,128)} %get-tuple-element.27) | copy-start | bytes 884740
  183.4 4.9 %copy-start = (bf16[4,202,768]{2,1,0:T(8,128)(2,1)S(1)}, bf16[4,202,768]{2,1,0:T(8,128)(2,1)}, u32[]{:S(2)}) copy-start(bf16[4,202,768]{2,1,0:T(8,128)(2,1)} %get-tuple-element.31) | copy-start | bytes 3723268
  188.3 1.7 copy-start.3
  188.3 2.4 %copy-start.2 = (f32[96,768]{1,0:T(8,128)S(1)}, f32[96,768]{1,0:T(8,128)}, u32[]{:S(2)}) copy-start(f32[96,768]{1,0:T(8,128)} %get-tuple-element.95) | copy-start | bytes 884740
